TPU v7x, 512 devices: a whole 4x4x16 slice. The times are simulated.
512 devices in a mesh: pipe: 128 (over y, z, x_lo), seq: 4 (over x_hi, core).
Axes of the slice: x: 4 (x_hi: 2, x_lo: 2; x = x_hi * 2 + x_lo), y: 4, z: 16, core: 2. Of those that a mesh axis runs over, the one named last changes fastest.
Arguments:
- activations: bfloat16 [32768, 3072], P(('pipe', 'seq')), may hold values from -200 to 200
- key_cache: bfloat16 [128, 1024, 1536], P('pipe', None, 'seq'), may hold values from -30 to 30
- value_cache: bfloat16 [128, 1024, 1536], P('pipe', None, 'seq'), may hold values from -6 to 6
- w_out: bfloat16 [128, 1536, 3072], P('pipe', 'seq'), may hold values from -0.15625 to 0.15625
- mod_shift: float32 [128, 3072], P('pipe'), may hold values from -3 to 3
- mod_scale: float32 [128, 3072], P('pipe'), may hold values from -2.5 to 2.5
- mod_gate: float32 [128, 3072], P('pipe'), may hold values from -12 to 12
- q_gain: float32 [128, 128], P('pipe'), may hold values from 0.5 to 6
- k_gain: float32 [128, 128], P('pipe'), may hold values from 0.5 to 6
- lengths: int32 [4], replicated, may hold values from 1 to 256, 960 in all
- first_patch: int32 [1], replicated, may hold values from 0 to 16383
Outputs:
- carried: bfloat16 [32768, 3072], P(('pipe', 'seq'))
Inputs may be any that keep to these rules, and one draw needn't show every extreme that they name: `lengths`: in sequence order; they sum to 960 and the longest is exactly 256.
All inputs are finite; a program needn't handle non-finite values.
Results may differ from a plain program's by a relative error of at most 0.018.
Values may be sent and summed in bfloat16 or wider, within the bound.
A program may use at most 64 MiB of HBM per device.

v0:
```python
import jax
import jax.numpy as jnp
from jax import lax
from jax.sharding import PartitionSpec as P

NP = 4
TICKS = 2


epsilon = 1e-06
masked_score = -1e30


def shifted(shard, axis, by):
    peers = lax.axis_size(axis)
    return lax.ppermute(shard, axis, [(i, (i + by) % peers) for i in range(peers)])


def refresh(stored, fresh_rows, first_row, length):
    total_rows = stored.shape[0]
    padded = jnp.zeros((total_rows + fresh_rows.shape[0], stored.shape[1]), stored.dtype)
    placed = lax.dynamic_update_slice(padded, fresh_rows, (first_row, jnp.int32(0)))[:total_rows]
    row_index = jnp.arange(total_rows, dtype=jnp.int32)
    inside = (row_index >= first_row) & (row_index < first_row + length)
    return jnp.where(inside[:, None], placed, stored)


def modulate(values, shift_row, scale_row):
    row_mean = jnp.mean(values, axis=1, keepdims=True)
    centred = values - row_mean
    variance = jnp.mean(centred * centred, axis=1, keepdims=True)
    return (centred / jnp.sqrt(variance + epsilon) * (1.0 + scale_row) + shift_row).astype(
        jnp.bfloat16
    )


def attend(head_input, key_store, value_store, query_gain, key_gain, first_row, length, live_count):
    patch_rows, local_width = head_input.shape
    head_size = query_gain.shape[0]
    head_count = local_width // head_size
    head_values = head_input.astype(jnp.float32).reshape(patch_rows, head_count, head_size)
    head_rms = jnp.sqrt(jnp.mean(head_values * head_values, axis=2, keepdims=True) + epsilon)
    normed = head_values / head_rms
    queries = (normed * query_gain).astype(jnp.bfloat16)
    fresh_keys = (normed * key_gain).astype(jnp.bfloat16).reshape(patch_rows, local_width)
    key_store = refresh(key_store, fresh_keys, first_row, length)
    value_store = refresh(value_store, head_input, first_row, length)
    capacity = key_store.shape[0]
    live_keys = jnp.arange(capacity, dtype=jnp.int32) < live_count
    key_heads = key_store.reshape(capacity, head_count, head_size)
    value_heads = value_store.reshape(capacity, head_count, head_size)

    def one_head(head_index):
        query_part = lax.dynamic_index_in_dim(queries, head_index, 1, keepdims=False)
        key_part = lax.dynamic_index_in_dim(key_heads, head_index, 1, keepdims=False)
        value_part = lax.dynamic_index_in_dim(value_heads, head_index, 1, keepdims=False)
        scores = lax.dot_general(
            query_part, key_part, (((1,), (1,)), ((), ())), preferred_element_type=jnp.float32
        ) * head_size ** (-0.5)
        scores = jnp.where(live_keys[None, :], scores, masked_score)
        row_max = jnp.max(scores, axis=1, keepdims=True)
        weight = jnp.exp(scores - row_max)
        probability = (weight / jnp.sum(weight, axis=1, keepdims=True)).astype(jnp.bfloat16)
        return jnp.dot(probability, value_part, preferred_element_type=jnp.float32).astype(
            jnp.bfloat16
        )

    attended = lax.map(one_head, jnp.arange(head_count, dtype=jnp.int32))
    attended = jnp.transpose(attended, (1, 0, 2)).reshape(patch_rows, local_width)
    return (attended, key_store, value_store)


def shards(
    activations,
    key_cache,
    value_cache,
    w_out,
    mod_shift,
    mod_scale,
    mod_gate,
    q_gain,
    k_gain,
    lengths,
    first_patch,
):
    seq_place = lax.axis_index("seq")
    section = lax.axis_index("pipe")
    local_rows, width = activations.shape
    local_width = key_cache.shape[2]
    capacity = key_cache.shape[1]
    live_count = capacity - local_rows
    first_rows = jnp.cumsum(lengths) - lengths
    shift_row = mod_shift[0]
    scale_row = mod_scale[0]
    gate_row = mod_gate[0]
    query_gain = q_gain[0]
    key_gain = k_gain[0]
    out_local = w_out[0]
    head_total = local_width * lax.axis_size("seq")

    def patch_of(segment_step):
        patch_id = (first_patch[0] + segment_step - section) % NP
        return (first_rows[patch_id], lengths[patch_id])

    def advance_tokens(segment_step, carry):
        carried, key_store, value_store = carry
        first_row, length = patch_of(segment_step)
        values = carried.astype(jnp.float32)
        modded = modulate(values, shift_row, scale_row)
        head_layout = lax.all_to_all(
            modded[:, :head_total], "seq", split_axis=1, concat_axis=0, tiled=True
        )
        attended, key_store, value_store = attend(
            head_layout, key_store, value_store, query_gain, key_gain, first_row, length, live_count
        )
        projected = lax.psum_scatter(
            jnp.dot(attended, out_local, preferred_element_type=jnp.float32).astype(jnp.bfloat16),
            "seq",
            scatter_dimension=0,
            tiled=True,
        ).astype(jnp.float32)
        updated = values + gate_row * projected
        row_index = seq_place * local_rows + jnp.arange(local_rows, dtype=jnp.int32)
        updated = jnp.where((row_index < length)[:, None], updated, 0.0).astype(jnp.bfloat16)
        passed = shifted(updated, "pipe", 1)
        return (passed, key_store, value_store)

    final_state = lax.fori_loop(
        0, TICKS, advance_tokens, (activations, key_cache[0], value_cache[0])
    )
    result = final_state[0]
    return result


def solution(mesh):
    in_specs = (
        P(("pipe", "seq"), None),
        P("pipe", None, "seq"),
        P("pipe", None, "seq"),
        P("pipe", "seq", None),
        P("pipe", None),
        P("pipe", None),
        P("pipe", None),
        P("pipe", None),
        P("pipe", None),
        P(),
        P(),
    )
    out_specs = P(("pipe", "seq"), None)
    return jax.shard_map(shards, mesh=mesh, in_specs=in_specs, out_specs=out_specs, check_vma=False)
```

profile of v0, /device:TPU:1, one launch (start us, length us, event | category | flops | bytes accessed | tf_op | source)
XLA Modules:
  0.0 242.8 jit_solution(7949313480583929229)
XLA Ops:
  6.6 0.9 reduce-window.9
  7.5 0.7 bitcast_subtract_fusion
  8.2 1.4 copy.57
  9.6 1.2 copy.58
  10.8 224.4 %while.52 = (s32[]{:T(128)}, bf16[64,3072]{1,0:T(8,128)(2,1)S(1)}, bf16[1024,384]{0,1:T(8,128)(2,1)S(1)}, bf16[1024,384]{0,1:T(8,128)(2,1)}, s32[]{:T(128)}, /*i...) while((s32[]{:T(128)}, bf16[64,3072]{1,0:T(8,128)(2,1)S(1)}, ...), condition=%wide.region_10.11_spmd, body=%wide.region_1.10_spmd.sunk | while | flops 745643456 | bytes 33083332 | solution.py:128
  11.4 0.7 copy.75
  12.1 10.2 %all-to-all-start = ((bf16[64,4,384]{2,0,1:T(8,128)(2,1)}), bf16[64,4,384]{2,0,1:T(8,128)(2,1)S(1)}, u32[]{:S(2)}, u32[]{:S(2)}) async-start(bf16[64,4,384]{2,0,1:T(8,128)(2,1)} %bitcast.82), calls=%async_computation | async-start | bytes 393216 | tf_op jit(solution)/shard_map/while/body/eval_jaxpr/all_to_all | solution.py:110
  23.0 0.7 dynamic_slice.62
  23.7 0.6 dynamic_slice.61
  27.5 0.6 fusion.34
  28.7 0.3 multiply_reduce_fusion.5
  29.3 0.3 multiply_convert_fusion.4
  30.1 1.0 broadcast.203.clone
  31.1 3.6 %dynamic_update_slice.29 = bf16[1280,384]{0,1:T(8,128)(2,1)} dynamic-update-slice(bf16[1280,384]{0,1:T(8,128)(2,1)} %broadcast.203.clone, bf16[256,384]{0,1:T(8,128)(2,1)S(1)} %copy.79, s32[]{:T(128)S(6)} %select_n.103, s32[]{:T(128)} %copy.108) | dynamic-update-slice | bytes 393220 | tf_op jit(solution)/shard_map/while/body/eval_jaxpr/dynamic_update_slice | solution.py:22
  34.8 3.3 %dynamic_update_slice.30 = bf16[1280,384]{0,1:T(8,128)(2,1)S(1)} dynamic-update-slice(bf16[1280,384]{0,1:T(8,128)(2,1)S(1)} %broadcast.203.clone.1, bf16[256,384]{0,1:T(8,128)(2,1)S(1)} %copy.81, s32[]{:T(128)S(6)} %select_n.103, s32[]{:T(128)} %copy.108) | dynamic-update-slice | bytes 393220 | tf_op jit(solution)/shard_map/while/body/eval_jaxpr/dynamic_update_slice | solution.py:22
  38.1 2.6 %slice_select_fusion.3 = (bf16[1024,384]{0,1:T(8,128)(2,1)}, bf16[1024,384]{0,1:T(8,128)(2,1)S(1)}) fusion(bf16[1024,384]{0,1:T(8,128)(2,1)} %get-tuple-element.693, bf16[1280,384]{0,1:T(8,128)(2,1)} %dynamic_update_slice.29, pred[1024]{0:T(1024)(128)(4,1)S(1)} %fusion.34, bf16[1024,384]{0,1:T(8,128)(2,1)S(1)} %get-tuple-element.692, ...), kind=kLoop, calls=%fused_computation.24.clone.1 | loop fusion | flops 786432 | bytes 4719616 | tf_op jit(solution)/shard_map/while/body/eval_jaxpr/jit(_where)/select_n | solution.py:25
  40.7 14.1 %while.53 = (s32[]{:T(128)}, bf16[3,256,128]{1,2,0:T(8,128)(2,1)S(1)}, s32[3]{0:T(128)S(1)}, bf16[256,3,128]{2,0,1:T(8,128)(2,1)S(1)}, bf16[1024,3,128]{0,2,1:T(...) while((s32[]{:T(128)}, ...), condition=%wide.region_8.8_spmd.clone, body=%wide.region_5.7_spmd.clone.sunk | while | flops 136348160 | bytes 4071579 | solution.py:68
  40.7 0.6 dynamic_slice.66
  43.3 0.4 fusion.37
  43.7 0.3 fusion.38
  44.0 1.3 fusion.39
  45.4 0.6 dynamic_slice.66
  48.0 0.4 fusion.37
  48.4 0.3 fusion.38
  48.7 1.3 fusion.39
  50.2 0.6 dynamic_slice.66
  52.7 0.4 fusion.37
  53.1 0.3 fusion.38
  53.4 1.3 fusion.39
  54.9 3.8 %convolution_convert_fusion.3 = bf16[256,3072]{1,0:T(8,128)(2,1)} fusion(bf16[256,384]{0,1:T(8,128)(2,1)S(1)} %bitcast.109, bf16[384,3072]{1,0:T(8,128)(2,1)} %get-tuple-element.728), kind=kOutput, calls=%fused_computation.18.clone.1 | convolution fusion | flops 604766208 | bytes 4128768 | tf_op jit(solution)/shard_map/while/body/eval_jaxpr/dot_general | solution.py:117
  58.7 0.7 add_compare_fusion.2
  59.4 49.7 %reduce-scatter.2.cloned.1.call-done = bf16[64,3072]{1,0:T(8,128)(2,1)} async-done(((bf16[256,3072]{1,0:T(8,128)(2,1)}), bf16[64,3072]{1,0:T(8,128)(2,1)}) %reduce-scatter.2.cloned.1.call-update) | async-done | bytes 393232 | tf_op jit(solution)/shard_map/while/body/eval_jaxpr/reduce_scatter | solution.py:116
  109.1 1.1 fusion.35
  110.2 2.2 collective-permute-start
  112.4 14.5 %collective-permute-done = bf16[64,3072]{1,0:T(8,128)(2,1)S(1)} collective-permute-done((bf16[64,3072]{1,0:T(8,128)(2,1)S(1)}, bf16[64,3072]{1,0:T(8,128)(2,1)S(1)}, u32[]{:S(2)}, u32[]{:S(2)}) %collective-permute-start) | collective-permute-done | bytes 393248 | tf_op jit(solution)/shard_map/while/body/eval_jaxpr/ppermute | solution.py:16
  127.5 0.7 copy.75
  128.2 4.6 %all-to-all-start = ((bf16[64,4,384]{2,0,1:T(8,128)(2,1)}), bf16[64,4,384]{2,0,1:T(8,128)(2,1)S(1)}, u32[]{:S(2)}, u32[]{:S(2)}) async-start(bf16[64,4,384]{2,0,1:T(8,128)(2,1)} %bitcast.82), calls=%async_computation | async-start | bytes 393216 | tf_op jit(solution)/shard_map/while/body/eval_jaxpr/all_to_all | solution.py:110
  133.5 0.7 dynamic_slice.62
  134.2 0.6 dynamic_slice.61
  137.9 0.6 fusion.34
  139.1 0.3 multiply_reduce_fusion.5
  139.7 0.3 multiply_convert_fusion.4
  140.6 1.0 broadcast.203.clone
  141.6 3.3 %dynamic_update_slice.29 = bf16[1280,384]{0,1:T(8,128)(2,1)} dynamic-update-slice(bf16[1280,384]{0,1:T(8,128)(2,1)} %broadcast.203.clone, bf16[256,384]{0,1:T(8,128)(2,1)S(1)} %copy.79, s32[]{:T(128)S(6)} %select_n.103, s32[]{:T(128)} %copy.108) | dynamic-update-slice | bytes 393220 | tf_op jit(solution)/shard_map/while/body/eval_jaxpr/dynamic_update_slice | solution.py:22
  144.9 2.6 %dynamic_update_slice.30 = bf16[1280,384]{0,1:T(8,128)(2,1)S(1)} dynamic-update-slice(bf16[1280,384]{0,1:T(8,128)(2,1)S(1)} %broadcast.203.clone.1, bf16[256,384]{0,1:T(8,128)(2,1)S(1)} %copy.81, s32[]{:T(128)S(6)} %select_n.103, s32[]{:T(128)} %copy.108) | dynamic-update-slice | bytes 393220 | tf_op jit(solution)/shard_map/while/body/eval_jaxpr/dynamic_update_slice | solution.py:22
  147.5 2.6 %slice_select_fusion.3 = (bf16[1024,384]{0,1:T(8,128)(2,1)}, bf16[1024,384]{0,1:T(8,128)(2,1)S(1)}) fusion(bf16[1024,384]{0,1:T(8,128)(2,1)} %get-tuple-element.693, bf16[1280,384]{0,1:T(8,128)(2,1)} %dynamic_update_slice.29, pred[1024]{0:T(1024)(128)(4,1)S(1)} %fusion.34, bf16[1024,384]{0,1:T(8,128)(2,1)S(1)} %get-tuple-element.692, ...), kind=kLoop, calls=%fused_computation.24.clone.1 | loop fusion | flops 786432 | bytes 4719616 | tf_op jit(solution)/shard_map/while/body/eval_jaxpr/jit(_where)/select_n | solution.py:25
  150.1 14.1 %while.53 = (s32[]{:T(128)}, bf16[3,256,128]{1,2,0:T(8,128)(2,1)S(1)}, s32[3]{0:T(128)S(1)}, bf16[256,3,128]{2,0,1:T(8,128)(2,1)S(1)}, bf16[1024,3,128]{0,2,1:T(...) while((s32[]{:T(128)}, ...), condition=%wide.region_8.8_spmd.clone, body=%wide.region_5.7_spmd.clone.sunk | while | flops 136348160 | bytes 4071579 | solution.py:68
  150.1 0.6 dynamic_slice.66
  152.7 0.4 fusion.37
  153.1 0.3 fusion.38
  153.4 1.3 fusion.39
  154.8 0.6 dynamic_slice.66
  157.4 0.4 fusion.37
  158.1 1.3 fusion.39
  159.6 0.6 dynamic_slice.66
  162.1 0.4 fusion.37
  162.8 1.3 fusion.39
  164.3 3.8 %convolution_convert_fusion.3 = bf16[256,3072]{1,0:T(8,128)(2,1)} fusion(bf16[256,384]{0,1:T(8,128)(2,1)S(1)} %bitcast.109, bf16[384,3072]{1,0:T(8,128)(2,1)} %get-tuple-element.728), kind=kOutput, calls=%fused_computation.18.clone.1 | convolution fusion | flops 604766208 | bytes 4128768 | tf_op jit(solution)/shard_map/while/body/eval_jaxpr/dot_general | solution.py:117
  168.1 0.7 add_compare_fusion.2
  168.8 48.6 %reduce-scatter.2.cloned.1.call-done = bf16[64,3072]{1,0:T(8,128)(2,1)} async-done(((bf16[256,3072]{1,0:T(8,128)(2,1)}), bf16[64,3072]{1,0:T(8,128)(2,1)}) %reduce-scatter.2.cloned.1.call-update) | async-done | bytes 393232 | tf_op jit(solution)/shard_map/while/body/eval_jaxpr/reduce_scatter | solution.py:116
  217.4 1.1 fusion.35
  218.6 2.2 collective-permute-start
  220.8 14.4 %collective-permute-done = bf16[64,3072]{1,0:T(8,128)(2,1)S(1)} collective-permute-done((bf16[64,3072]{1,0:T(8,128)(2,1)S(1)}, bf16[64,3072]{1,0:T(8,128)(2,1)S(1)}, u32[]{:S(2)}, u32[]{:S(2)}) %collective-permute-start) | collective-permute-done | bytes 393248 | tf_op jit(solution)/shard_map/while/body/eval_jaxpr/ppermute | solution.py:16
  235.2 0.7 copy.109
  (88 shorter events, 5.2 us)
Async XLA Ops:
  6.5 4.2 %copy-start.7 = (s32[4]{0:T(128)S(1)}, s32[4]{0:T(128)}, u32[]{:S(2)}) copy-start(s32[4]{0:T(128)} %param.24) | copy-start | bytes 52
  6.5 4.2 %copy-start.6 = (f32[1,128]{1,0:T(1,128)S(1)}, f32[1,128]{1,0:T(1,128)}, u32[]{:S(2)}) copy-start(f32[1,128]{1,0:T(1,128)} %param.23) | copy-start | bytes 1540
  6.5 4.2 %copy-start.5 = (f32[1,128]{1,0:T(1,128)S(1)}, f32[1,128]{1,0:T(1,128)}, u32[]{:S(2)}) copy-start(f32[1,128]{1,0:T(1,128)} %param.22) | copy-start | bytes 1540
  6.5 4.2 %copy-start.2 = (f32[1,3072]{1,0:T(1,128)S(1)}, f32[1,3072]{1,0:T(1,128)}, u32[]{:S(2)}) copy-start(f32[1,3072]{1,0:T(1,128)} %param.21) | copy-start | bytes 36868
  6.5 4.2 %copy-start.3 = (f32[1,3072]{1,0:T(1,128)S(1)}, f32[1,3072]{1,0:T(1,128)}, u32[]{:S(2)}) copy-start(f32[1,3072]{1,0:T(1,128)} %param.20) | copy-start | bytes 36868
  6.5 4.2 %copy-start.4 = (f32[1,3072]{1,0:T(1,128)S(1)}, f32[1,3072]{1,0:T(1,128)}, u32[]{:S(2)}) copy-start(f32[1,3072]{1,0:T(1,128)} %param.19) | copy-start | bytes 36868
  6.6 3.0 %copy-start.1 = (bf16[1,1024,384]{2,1,0:T(8,128)(2,1)S(1)}, bf16[1,1024,384]{2,1,0:T(8,128)(2,1)}, u32[]{:S(2)}) copy-start(bf16[1,1024,384]{2,1,0:T(8,128)(2,1)} %param.17) | copy-start | bytes 2359300
  6.6 4.2 %copy-start = (bf16[64,3072]{1,0:T(8,128)(2,1)S(1)}, bf16[64,3072]{1,0:T(8,128)(2,1)}, u32[]{:S(2)}) copy-start(bf16[64,3072]{1,0:T(8,128)(2,1)} %param.15) | copy-start | bytes 1179652
  12.1 16.2 %all-to-all-start = ((bf16[64,4,384]{2,0,1:T(8,128)(2,1)}), bf16[64,4,384]{2,0,1:T(8,128)(2,1)S(1)}, u32[]{:S(2)}, u32[]{:S(2)}) async-start(bf16[64,4,384]{2,0,1:T(8,128)(2,1)} %bitcast.82), calls=%async_computation | async-start | bytes 393216 | tf_op jit(solution)/shard_map/while/body/eval_jaxpr/all_to_all | solution.py:110
  22.4 86.7 %reduce-scatter.2.cloned.1.call-start = ((), (), s32[]{:S(2)}) async-start(), calls=%async_computation.2 | async-start | bytes 1966080 | tf_op jit(solution)/shard_map/while/body/eval_jaxpr/reduce_scatter | solution.py:116
  110.2 16.7 %collective-permute-start = (bf16[64,3072]{1,0:T(8,128)(2,1)S(1)}, bf16[64,3072]{1,0:T(8,128)(2,1)S(1)}, u32[]{:S(2)}, u32[]{:S(2)}) collective-permute-start(bf16[64,3072]{1,0:T(8,128)(2,1)S(1)} %fusion.35), channel_id=1, source_target_pairs={{0,4},{4,8},{8,12},{12,16},{16,20},{20,24},{24,28},{28,32},{32,36}... | collective-permute-start | bytes 1179656 | tf_op jit(solution)/shard_map/while/body/eval_jaxpr/ppermute | solution.py:16
  128.2 10.5 %all-to-all-start = ((bf16[64,4,384]{2,0,1:T(8,128)(2,1)}), bf16[64,4,384]{2,0,1:T(8,128)(2,1)S(1)}, u32[]{:S(2)}, u32[]{:S(2)}) async-start(bf16[64,4,384]{2,0,1:T(8,128)(2,1)} %bitcast.82), calls=%async_computation | async-start | bytes 393216 | tf_op jit(solution)/shard_map/while/body/eval_jaxpr/all_to_all | solution.py:110
  132.8 84.6 %reduce-scatter.2.cloned.1.call-start = ((), (), s32[]{:S(2)}) async-start(), calls=%async_computation.2 | async-start | bytes 1966080 | tf_op jit(solution)/shard_map/while/body/eval_jaxpr/reduce_scatter | solution.py:116
  218.6 16.6 %collective-permute-start = (bf16[64,3072]{1,0:T(8,128)(2,1)S(1)}, bf16[64,3072]{1,0:T(8,128)(2,1)S(1)}, u32[]{:S(2)}, u32[]{:S(2)}) collective-permute-start(bf16[64,3072]{1,0:T(8,128)(2,1)S(1)} %fusion.35), channel_id=1, source_target_pairs={{0,4},{4,8},{8,12},{12,16},{16,20},{20,24},{24,28},{28,32},{32,36}... | collective-permute-start | bytes 1179656 | tf_op jit(solution)/shard_map/while/body/eval_jaxpr/ppermute | solution.py:16
Sparse Core Ops, SparseCore 0:
  58.8 50.2 reduce-scatter.1
  168.2 49.1 reduce-scatter.1
where the time goes:
time: 244 us; the launch traced here: 243 us
  waiting for transfers between devices  128 us (52%)
  local copies, waits for them, and re-layouts  28.3 us (12%)
  loops' own time  20 us (8%)
  starting transfers between devices  19.1 us (8%)
  matrix products  17.8 us (7%)
  other arithmetic  16.4 us (7%)
  between operations  13.5 us (6%)
    reduce_scatter x2, waiting for transfers between devices, advance_tokens(): lax.psum_scatter(jnp.dot(attended, out_local, preferred_element_type=jnp....  98.3 us
    ppermute x2, waiting for transfers between devices, shifted(): lax.ppermute(shard, axis, [(i, (i + by) % peers) for i in range(peers)])  28.9 us
    all_to_all x2, starting transfers between devices, advance_tokens(): lax.all_to_all(modded[:, :head_total], 'seq', split_axis=1, concat_axis=0...  14.8 us
    dynamic_update_slice x4, local copies, waits for them, and re-layouts, refresh(): lax.dynamic_update_slice(padded, fresh_rows, (first_row, jnp.int32(0)))  12.8 us
    another operation x2, loops' own time, attend(): attended = lax.map(one_head, jnp.arange(head_count, dtype=jnp.int32))  11.9 us
    another operation x1, loops' own time, shards(): lax.fori_loop(0, TICKS, advance_tokens, (activations, key_cache[0], value...  8.13 us
    dot_general x6, matrix products, one_head(): jnp.dot(probability, value_part, preferred_element_type=jnp.float32)  7.92 us
    dot_general x2, matrix products, advance_tokens(): jnp.dot(attended, out_local, preferred_element_type=jnp.float32)  7.65 us
  transfers between devices with their start and end apart: 6, of which 6 were waited for; matrix products, arithmetic and copies ran while one was open for 2% of the time, Pallas kernels for 0%

commit v1 on v0

v1 whole, which is shorter than its diff:
```python
import functools
import math

import jax
import jax.numpy as jnp
from jax import lax
from jax.experimental import pallas as pl
from jax.experimental.pallas import tpu as pltpu
from jax.sharding import PartitionSpec as P

MESH = pl.DeviceIdType.MESH
BF16 = jnp.bfloat16
F32 = jnp.float32

NP = 4
EPS = 1e-06
MASKED = -1e30
HD = 128
BLK = 384
SLAB = 2 * BLK
ROWS = 64
PATCH = 256
CAP = 1024
TOTAL = 960
WIDTH = 3072
HALF = WIDTH // 2
EXP2_SCALE = math.log2(math.e) / math.sqrt(HD)


def mult(value, of):
    return pl.multiple_of(value, of)


def kernel(
    n_pipe,
    x_hbm,
    k_hbm,
    v_hbm,
    w_hbm,
    shift_hbm,
    scale_hbm,
    gate_hbm,
    qg_hbm,
    kg_hbm,
    lengths,
    first_patch,
    out_hbm,
    xv,
    kv,
    vv,
    w4,
    shv,
    scv,
    gav,
    qgv,
    kgv,
    xh,
    st1,
    res,
    qb,
    fh,
    att1,
    sb1,
    rb,
    xs,
    st2,
    rx,
    as2,
    att2,
    sb2,
    lsem,
    xh_s,
    xh_r,
    st_s,
    st_r,
    res_s,
    res_r,
    w_s,
    w_r,
    a1_s,
    a1_r,
    p1_s,
    p1_r,
    s2_s,
    s2_r,
    rx_s,
    rx_r,
    a2_s,
    a2_r,
    p2_s,
    p2_r,
):
    s = lax.axis_index("pipe")
    q = lax.axis_index("seq")
    j = q // 2
    c = q % 2
    nxt = (s + 1) % n_pipe
    prv = (s + n_pipe - 1) % n_pipe
    chip = [j, 1 - j]
    slab = [2 * chip[0] + c, 2 * chip[1] + c]
    mate_slab = [2 * chip[0] + (1 - c), 2 * chip[1] + (1 - c)]
    peer = {1: mate_slab[0], 2: slab[1], 3: mate_slab[1]}
    mate = peer[1]

    def remote(src, dst, ssem, rsem, pipe, seq):
        return pltpu.make_async_remote_copy(
            src_ref=src,
            dst_ref=dst,
            send_sem=ssem,
            recv_sem=rsem,
            device_id={"pipe": pipe, "seq": seq},
            device_id_type=MESH,
        )

    local = []

    def load(src, dst):
        copy = pltpu.make_async_copy(src, dst, lsem.at[len(local)])
        copy.start()
        local.append(copy)
        return copy

    ld_x = load(x_hbm, xv)
    ld_small = [
        load(shift_hbm, shv),
        load(scale_hbm, scv),
        load(gate_hbm, gav),
        load(qg_hbm, qgv),
        load(kg_hbm, kgv),
    ]
    ld_xh = load(x_hbm.at[:, pl.ds(mult(BLK * q, 128), BLK)], xh.at[pl.ds(mult(ROWS * q, ROWS), ROWS)])
    ld_k = load(k_hbm.at[0], kv)
    ld_v = load(v_hbm.at[0], vv)

    bar = pltpu.get_barrier_semaphore()
    for k in (1, 2, 3):
        pl.semaphore_signal(bar, inc=1, device_id={"pipe": s, "seq": peer[k]}, device_id_type=MESH)
    for v in (0, 1):
        pl.semaphore_signal(bar, inc=1, device_id={"pipe": prv, "seq": slab[v]}, device_id_type=MESH)
    pl.semaphore_wait(bar, 5)

    xh_copies = {}
    for k in (2, 3, 1):
        xh_copies[k] = remote(
            x_hbm.at[:, pl.ds(mult(BLK * peer[k], 128), BLK)],
            xh.at[pl.ds(mult(ROWS * q, ROWS), ROWS)],
            xh_s.at[k - 1],
            xh_r.at[k - 1],
            s,
            peer[k],
        )
        xh_copies[k].start()

    ld_res = []
    res_copies = []
    for v in (0, 1):
        for e in (0, 1):
            dst = res.at[v, pl.ds(mult(ROWS * c, ROWS), ROWS), pl.ds(BLK * e, BLK)]
            ld_res.append(load(x_hbm.at[:, pl.ds(mult(HALF * e + BLK * slab[v], 128), BLK)], dst))
            copy = remote(
                x_hbm.at[:, pl.ds(mult(HALF * e + BLK * mate_slab[v], 128), BLK)],
                dst,
                res_s.at[2 * v + e],
                res_r.at[2 * v + e],
                s,
                mate,
            )
            copy.start()
            res_copies.append(copy)

    ld_w = []
    w_copies = []
    for n, (mine, his) in enumerate(
        [(slab[0], mate_slab[0]), (slab[1], mate_slab[1]), (mate_slab[0], slab[0]), (mate_slab[1], slab[1])]
    ):
        for e in (0, 1):
            for g, away in ((mine, False), (his, True)):
                src = w_hbm.at[0, :, pl.ds(mult(HALF * e + BLK * g, 128), BLK)]
                dst = w4.at[g, pl.ds(mult(BLK * c, BLK), BLK), pl.ds(BLK * e, BLK)]
                if away:
                    copy = remote(src, dst, w_s.at[2 * n + e], w_r.at[2 * n + e], s, mate)
                    copy.start()
                    w_copies.append(copy)
                else:
                    ld_w.append(load(src, dst))

    ld_x.wait()
    xf = xv[...].astype(F32)
    mean = jnp.sum(xf, axis=1, keepdims=True) * (1.0 / WIDTH)
    cent = xf - mean
    var = jnp.sum(cent * cent, axis=1, keepdims=True) * (1.0 / WIDTH)
    rstd = lax.rsqrt(var + EPS)
    lane = lax.broadcasted_iota(jnp.int32, (ROWS, 128), 1)
    st1[pl.ds(mult(ROWS * q, ROWS), ROWS), :] = jnp.where(lane == 0, mean, rstd)
    st_copies = {}
    for k in (2, 3, 1):
        part = st1.at[pl.ds(mult(ROWS * q, ROWS), ROWS)]
        st_copies[k] = remote(part, part, st_s.at[k - 1], st_r.at[k - 1], s, peer[k])
        st_copies[k].start()

    for copy in ld_small:
        copy.wait()
    scale_h = 1.0 + scv[:, pl.ds(mult(BLK * q, 128), BLK)]
    shift_h = shv[:, pl.ds(mult(BLK * q, 128), BLK)]
    q_gain = qgv[...]
    k_gain = kgv[...]

    def patch_at(t):
        p = (first_patch[0] + t + n_pipe * NP - s) % NP
        first = jnp.int32(0)
        length = jnp.int32(0)
        for n in range(NP):
            first = first + jnp.where(n < p, lengths[n], 0)
            length = length + jnp.where(n == p, lengths[n], 0)
        return first, length

    def prep_rows(raw, mean, rstd, rows):
        modded = ((raw - mean) * rstd * scale_h + shift_h).astype(BF16)
        fh[rows, BLK:] = modded
        mf = modded.astype(F32)
        for h in range(BLK // HD):
            part = mf[:, HD * h : HD * (h + 1)]
            rms = jnp.sqrt(jnp.mean(part * part, axis=1, keepdims=True) + EPS)
            normed = part / rms
            qb[rows, HD * h : HD * (h + 1)] = (normed * q_gain).astype(BF16)
            fh[rows, HD * h : HD * (h + 1)] = (normed * k_gain).astype(BF16)

    def refresh(first, length):
        def block(n, carry):
            rows = pl.ds(mult(n * PATCH, PATCH), PATCH)
            row = lax.broadcasted_iota(jnp.int32, (PATCH, PATCH), 0) + n * PATCH
            col = lax.broadcasted_iota(jnp.int32, (PATCH, PATCH), 1)
            pick = jnp.where((row - first == col) & (col < length), 1.0, 0.0).astype(BF16)
            placed = jnp.dot(pick, fh[...], preferred_element_type=F32)
            at = lax.broadcasted_iota(jnp.int32, (PATCH, BLK), 0) + n * PATCH
            inside = (at >= first) & (at < first + length)
            kv[rows, :] = jnp.where(inside, placed[:, :BLK], kv[rows, :].astype(F32)).astype(BF16)
            vv[rows, :] = jnp.where(inside, placed[:, BLK:], vv[rows, :].astype(F32)).astype(BF16)
            return carry

        lax.fori_loop(0, CAP // PATCH, block, 0)

    def attend(queries, live):
        parts = []
        for h in range(BLK // HD):
            cols = slice(HD * h, HD * (h + 1))
            scores = lax.dot_general(
                queries[:, cols], kv[:, cols], (((1,), (1,)), ((), ())), preferred_element_type=F32
            )
            rows = scores.shape[0]
            tail = CAP - 128
            at = lax.broadcasted_iota(jnp.int32, (rows, 128), 1) + tail
            scores = jnp.concatenate(
                [scores[:, :tail], jnp.where(at < TOTAL, scores[:, tail:], MASKED)], axis=1
            )
            top = jnp.max(scores, axis=1, keepdims=True)
            weight = jnp.exp2((scores - top) * EXP2_SCALE)
            total = jnp.sum(weight, axis=1, keepdims=True)
            out = jnp.dot(weight.astype(BF16), vv[:, cols], preferred_element_type=F32)
            parts.append(jnp.where(live, out / total, 0.0).astype(BF16))
        return jnp.concatenate(parts, axis=1)

    def gates(g):
        lo = gav[:, pl.ds(mult(BLK * g, 128), BLK)]
        hi = gav[:, pl.ds(mult(HALF + BLK * g, 128), BLK)]
        return jnp.concatenate([lo, hi], axis=1)

    own_cols = pl.ds(mult(BLK * c, BLK), BLK)

    first, length = patch_at(0)
    for k in (1, 2, 3):
        xh_copies[k].wait_recv()
    ld_xh.wait()
    for k in (1, 2, 3):
        st_copies[k].wait_recv()

    def prep0(n, carry):
        rows = pl.ds(mult(n * ROWS, ROWS), ROWS)
        stat = st1[rows, :]
        prep_rows(xh[rows, :].astype(F32), stat[:, 0:1], stat[:, 1:2], rows)
        return carry

    lax.fori_loop(0, PATCH // ROWS, prep0, 0)
    ld_k.wait()
    ld_v.wait()
    refresh(first, length)

    def att1_copy(i):
        part = att1.at[pl.ds(mult(i * ROWS, ROWS), ROWS), own_cols]
        return remote(part, part, a1_s.at[i], a1_r.at[i], s, mate)

    def p1_copy(i, v):
        rows = pl.ds(mult(i * ROWS, ROWS), ROWS)
        return remote(sb1.at[v, rows], rb.at[v, rows], p1_s.at[v, i], p1_r.at[v, i], nxt, slab[v])

    for copy in ld_res:
        copy.wait()
    for copy in res_copies:
        copy.wait_recv()
    for copy in ld_w[:4]:
        copy.wait()
    for copy in w_copies[:4]:
        copy.wait_recv()

    gate1 = [gates(slab[0]), gates(slab[1])]

    def step0(i, carry):
        @pl.when(i < PATCH // ROWS)
        def _():
            rows = pl.ds(mult(i * ROWS, ROWS), ROWS)
            live = lax.broadcasted_iota(jnp.int32, (ROWS, HD), 0) + i * ROWS < length
            att1[rows, own_cols] = attend(qb[rows, :], live)
            att1_copy(i).start()

        @pl.when(i > 0)
        def _():
            n = i - 1
            att1_copy(n).wait_recv()
            rows = pl.ds(mult(n * ROWS, ROWS), ROWS)
            live = lax.broadcasted_iota(jnp.int32, (ROWS, SLAB), 0) + n * ROWS < length
            keep = live & (n // 2 == j)
            for v in (0, 1):
                proj = jnp.dot(att1[rows, :], w4[slab[v]], preferred_element_type=F32)
                held = res[v, pl.ds(mult((n % 2) * ROWS, ROWS), ROWS), :].astype(F32)
                sb1[v, rows, :] = (proj * gate1[v] + jnp.where(keep, held, 0.0)).astype(BF16)
                p1_copy(n, v).start()

        return carry

    lax.fori_loop(0, PATCH // ROWS + 1, step0, 0)

    st2[0] = jnp.zeros((ROWS, 128), F32)

    def take(i, carry):
        rows = pl.ds(mult(i * ROWS, ROWS), ROWS)
        for v in (0, 1):
            p1_copy(i, v).wait_recv()
        held = (rb[0, rows, :].astype(F32) + rb[1, rows, :].astype(F32)).astype(BF16)
        xs[rows, :] = held
        hf = held.astype(F32)
        mean = jnp.sum(hf, axis=1, keepdims=True) * (1.0 / SLAB)
        cent = hf - mean
        spread = jnp.sum(cent * cent, axis=1, keepdims=True)
        st2[0] = jnp.where(lane == 2 * i, mean, jnp.where(lane == 2 * i + 1, spread, st2[0]))
        return carry

    lax.fori_loop(0, PATCH // ROWS, take, 0)
    s2_copies = {}
    for k in (2, 3, 1):
        s2_copies[k] = remote(st2.at[0], st2.at[k], s2_s.at[k - 1], s2_r.at[k - 1], s, peer[k])
        s2_copies[k].start()
    rx_copies = []
    for v in (0, 1):
        src = xs.at[pl.ds(mult(ROWS * mate_slab[v], ROWS), ROWS)]
        copy = remote(src, rx.at[v], rx_s.at[v], rx_r.at[v], s, mate)
        copy.start()
        rx_copies.append(copy)

    first, length = patch_at(1)
    for k in (1, 2, 3):
        s2_copies[k].wait_recv()
    stats = [st2[k] for k in range(4)]
    for i in range(PATCH // ROWS):
        means = [stat[:, 2 * i : 2 * i + 1] for stat in stats]
        spreads = [stat[:, 2 * i + 1 : 2 * i + 2] for stat in stats]
        mean = (means[0] + means[1] + means[2] + means[3]) * 0.25
        spread = spreads[0] + spreads[1] + spreads[2] + spreads[3]
        for m in means:
            spread = spread + (m - mean) * (m - mean) * SLAB
        rstd = lax.rsqrt(spread * (1.0 / WIDTH) + EPS)
        rows = slice(i * ROWS, (i + 1) * ROWS)
        prep_rows(xs[rows, :BLK].astype(F32), mean, rstd, rows)

    refresh(first, length)

    half = ROWS // 2

    def att2_copy(i):
        rows = pl.ds(mult(i * ROWS, ROWS), ROWS)
        return remote(as2.at[rows], att2.at[rows, own_cols], a2_s.at[i], a2_r.at[i], s, mate)

    def p2_copy(i, v):
        rows = pl.ds(mult(i * half, half), half)
        return remote(sb2.at[v, rows], out_hbm.at[v, rows], p2_s.at[v, i], p2_r.at[v, i], nxt, slab[v])

    for copy in rx_copies:
        copy.wait_recv()
    for copy in ld_w[4:]:
        copy.wait()
    for copy in w_copies[4:]:
        copy.wait_recv()

    bases = [ROWS * slab[0], ROWS * slab[1], ROWS * mate_slab[0], ROWS * mate_slab[1]]
    order = [slab[0], mate_slab[0], slab[1], mate_slab[1]]

    def step1(i, carry):
        @pl.when(i < 2)
        def _():
            queries = jnp.concatenate(
                [qb[pl.ds(mult(base + half * i, half), half), :] for base in bases], axis=0
            )
            r = lax.broadcasted_iota(jnp.int32, (4 * half, HD), 0)
            seg = r // half
            base = jnp.where(
                seg == 0, bases[0], jnp.where(seg == 1, bases[1], jnp.where(seg == 2, bases[2], bases[3]))
            )
            live = base + half * i + r % half < length
            got = attend(queries, live)
            rows = pl.ds(mult(i * ROWS, ROWS), ROWS)
            att2[rows, own_cols] = got[:ROWS]
            as2[rows, :] = got[ROWS:]
            att2_copy(i).start()

        @pl.when(i > 0)
        def _():
            n = i - 1
            att2_copy(n).wait_recv()
            rows = pl.ds(mult(n * ROWS, ROWS), ROWS)
            part = pl.ds(mult(n * half, half), half)
            left = att2[rows, :]
            for at, g in enumerate(order):
                proj = jnp.dot(left, w4[g], preferred_element_type=F32) * gates(g)
                if at == 0:
                    proj = proj + jnp.concatenate(
                        [xs[pl.ds(mult(base + half * n, half), half), :] for base in bases[:2]], axis=0
                    ).astype(F32)
                if at == 1:
                    proj = proj + jnp.concatenate([rx[0, part, :], rx[1, part, :]], axis=0).astype(F32)
                proj = proj.astype(BF16)
                for v in (0, 1):
                    for e in (0, 1):
                        sb2[v, part, pl.ds(mult(HALF * e + BLK * g, 128), BLK)] = proj[
                            v * half : (v + 1) * half, e * BLK : (e + 1) * BLK
                        ]
            for v in (0, 1):
                p2_copy(n, v).start()

        return carry

    lax.fori_loop(0, 3, step1, 0)

    for k in (1, 2, 3):
        xh_copies[k].wait_send()
        st_copies[k].wait_send()
        s2_copies[k].wait_send()
    for copy in res_copies + w_copies + rx_copies:
        copy.wait_send()
    for i in range(PATCH // ROWS):
        att1_copy(i).wait_send()
        for v in (0, 1):
            p1_copy(i, v).wait_send()
    for i in range(2):
        att2_copy(i).wait_send()
        for v in (0, 1):
            p2_copy(i, v).wait()


def shards(n_pipe, *args):
    dma = pltpu.SemaphoreType.DMA
    any_space = pl.BlockSpec(memory_space=pl.ANY)
    hbm = pl.BlockSpec(memory_space=pltpu.HBM)
    smem = pl.BlockSpec(memory_space=pltpu.SMEM)
    chunks = PATCH // ROWS
    parts = pl.pallas_call(
        functools.partial(kernel, n_pipe),
        out_shape=jax.ShapeDtypeStruct((2, ROWS, WIDTH), BF16),
        in_specs=[hbm] * 9 + [smem] * 2,
        out_specs=any_space,
        scratch_shapes=[
            pltpu.VMEM((ROWS, WIDTH), BF16),
            pltpu.VMEM((CAP, BLK), BF16),
            pltpu.VMEM((CAP, BLK), BF16),
            pltpu.VMEM((4, SLAB, SLAB), BF16),
            pltpu.VMEM((1, WIDTH), F32),
            pltpu.VMEM((1, WIDTH), F32),
            pltpu.VMEM((1, WIDTH), F32),
            pltpu.VMEM((1, HD), F32),
            pltpu.VMEM((1, HD), F32),
            pltpu.VMEM((PATCH, BLK), BF16),
            pltpu.VMEM((PATCH, 128), F32),
            pltpu.VMEM((2, 2 * ROWS, SLAB), BF16),
            pltpu.VMEM((PATCH, BLK), BF16),
            pltpu.VMEM((PATCH, SLAB), BF16),
            pltpu.VMEM((PATCH, SLAB), BF16),
            pltpu.VMEM((2, PATCH, SLAB), BF16),
            pltpu.VMEM((2, PATCH, SLAB), BF16),
            pltpu.VMEM((PATCH, SLAB), BF16),
            pltpu.VMEM((4, ROWS, 128), F32),
            pltpu.VMEM((2, ROWS, SLAB), BF16),
            pltpu.VMEM((2 * ROWS, BLK), BF16),
            pltpu.VMEM((2 * ROWS, SLAB), BF16),
            pltpu.VMEM((2, ROWS, WIDTH), BF16),
            dma((24,)),
            dma((3,)),
            dma((3,)),
            dma((3,)),
            dma((3,)),
            dma((4,)),
            dma((4,)),
            dma((8,)),
            dma((8,)),
            dma((chunks,)),
            dma((chunks,)),
            dma((2, chunks)),
            dma((2, chunks)),
            dma((3,)),
            dma((3,)),
            dma((2,)),
            dma((2,)),
            dma((2,)),
            dma((2,)),
            dma((2, 2)),
            dma((2, 2)),
        ],
        compiler_params=pltpu.CompilerParams(
            collective_id=0, has_side_effects=True, vmem_limit_bytes=40 << 20
        ),
        name="section_steps",
    )(*args)
    return (parts[0].astype(F32) + parts[1].astype(F32)).astype(BF16)


def solution(mesh):
    in_specs = (
        P(("pipe", "seq"), None),
        P("pipe", None, "seq"),
        P("pipe", None, "seq"),
        P("pipe", "seq", None),
        P("pipe", None),
        P("pipe", None),
        P("pipe", None),
        P("pipe", None),
        P("pipe", None),
        P(),
        P(),
    )
    return jax.shard_map(
        functools.partial(shards, mesh.shape["pipe"]),
        mesh=mesh,
        in_specs=in_specs,
        out_specs=P(("pipe", "seq"), None),
        check_vma=False,
    )
```

time: 244 us -> 78.7 us (0.32)
  waiting for transfers between devices: 128 us -> 0 us
  Pallas kernels: 0 us -> 67.8 us
  loops' own time: 20 us -> 0 us
  local copies, waits for them, and re-layouts: 28.3 us -> 9 us
  starting transfers between devices: 19.1 us -> 0 us
  matrix products: 17.8 us -> 0 us
  other arithmetic: 16.4 us -> 0.84 us
  between operations: 13.5 us -> 0.68 us
    reduce_scatter x2 -> x0, waiting for transfers between devices: 98.3 us -> none  [advance_tokens(): lax.psum_scatter(jnp.dot(attended, out_local, preferred_element_type=jnp....]
    pallas_call x0 -> x1, Pallas kernels: none -> 67.8 us  [shards(): pl.pallas_call(functools.partial(kernel, n_pipe), out_shape=jax.ShapeDtyp...]
    ppermute x2 -> x0, waiting for transfers between devices: 28.9 us -> none  [shifted(): lax.ppermute(shard, axis, [(i, (i + by) % peers) for i in range(peers)])]
    another operation x3 -> x0, loops' own time: 20 us -> none  [the longest x2 11.9 us: attend(): attended = lax.map(one_head, jnp.arange(head_count, dtype=jnp.int32))]
    dot_general x14 -> x0, matrix products: 17.8 us -> none  [the longest x6 7.92 us: one_head(): jnp.dot(probability, value_part, preferred_element_type=jnp.float32)]
    all_to_all x2 -> x0, starting transfers between devices: 14.8 us -> none  [advance_tokens(): lax.all_to_all(modded[:, :head_total], 'seq', split_axis=1, concat_axis=0...]
    dynamic_update_slice x16 -> x0, local copies, waits for them, and re-layouts: 13.5 us -> none  [the longest x4 12.8 us: refresh(): lax.dynamic_update_slice(padded, fresh_rows, (first_row, jnp.int32(0)))]
    dynamic_slice x10 -> x0, local copies, waits for them, and re-layouts: 6.04 us -> none  [the longest x6 3.51 us: attend(): attended = lax.map(one_head, jnp.arange(head_count, dtype=jnp.int32))]
  transfers between devices with their start and end apart: 6 -> 0, of which waited for: 6 -> 0; matrix products, arithmetic and copies ran while one was open for 2% -> 0% of each run, Pallas kernels for 0% -> 0%
where the time goes in v1:
time: 78.7 us; the launch traced here: 78.3 us
  Pallas kernels  67.8 us (86%)
  local copies, waits for them, and re-layouts  9 us (11%)
  other arithmetic  0.84 us (1%)
    pallas_call x1, Pallas kernels, shards(): pl.pallas_call(functools.partial(kernel, n_pipe), out_shape=jax.ShapeDtyp...  67.8 us
    unnamed x20, local copies, waits for them, and re-layouts  9 us

profile of v1, /device:TPU:1, one launch (start us, length us, event | category | flops | bytes accessed | tf_op | source)
XLA Modules:
  0.0 78.3 jit_solution(6801567380968021025)
XLA Ops:
  0.7 0.0 copy-start
  0.7 1.7 %copy-done = bf16[1,384,3072]{2,1,0:T(8,128)(2,1)S(1)} copy-done((bf16[1,384,3072]{2,1,0:T(8,128)(2,1)S(1)}, bf16[1,384,3072]{2,1,0:T(8,128)(2,1)}, u32[]{:S(2)}) %copy-start) | copy-done | bytes 2359320
  2.3 0.0 copy-start.1
  2.3 1.1 %copy-done.1 = bf16[1,1024,384]{2,1,0:T(8,128)(2,1)S(1)} copy-done((bf16[1,1024,384]{2,1,0:T(8,128)(2,1)S(1)}, bf16[1,1024,384]{2,1,0:T(8,128)(2,1)}, u32[]{:S(2)}) %copy-start.1) | copy-done | bytes 786456
  3.5 0.0 copy-start.2
  3.5 1.1 %copy-done.2 = bf16[1,1024,384]{2,1,0:T(8,128)(2,1)S(1)} copy-done((bf16[1,1024,384]{2,1,0:T(8,128)(2,1)S(1)}, bf16[1,1024,384]{2,1,0:T(8,128)(2,1)}, u32[]{:S(2)}) %copy-start.2) | copy-done | bytes 786456
  4.6 0.0 copy-start.3
  4.6 1.0 %copy-done.3 = bf16[64,3072]{1,0:T(8,128)(2,1)S(1)} copy-done((bf16[64,3072]{1,0:T(8,128)(2,1)S(1)}, bf16[64,3072]{1,0:T(8,128)(2,1)}, u32[]{:S(2)}) %copy-start.3) | copy-done | bytes 393240
  5.6 0.0 copy-start.4
  5.6 0.7 copy-done.4
  6.3 0.0 copy-start.5
  6.3 0.7 copy-done.5
  7.0 0.0 copy-start.6
  7.0 0.7 copy-done.6
  7.7 0.0 copy-start.7
  7.7 0.7 copy-done.7
  8.4 0.0 copy-start.8
  8.4 0.7 copy-done.8
  9.0 0.0 copy-start.9
  9.0 0.7 copy-done.9
  9.7 67.8 %section_steps.1 = bf16[2,64,3072]{2,1,0:T(8,128)(2,1)S(1)} custom-call(bf16[64,3072]{1,0:T(8,128)(2,1)S(1)} %copy-done.3, bf16[1,1024,384]{2,1,0:T(8,128)(2,1)S(1)} %copy-done.1, bf16[1,1024,384]{2,1,0:T(8,128)(2,1)S(1)} %copy-done.2, bf16[1,384,3072]{2,1,0:T(8,128)(2,1)S(1)} %copy-done, f32[1,3072]{1,0:T(1,128)S(1)} %copy-done.4, f32[1,3072]{1,0:T(1,128)S(1)} %copy-done.5, ...), custom_call_target="tpu_custom_call" | custom-call | tf_op jit(solution)/shard_map/section_steps/pallas_call | solution.py:464
  77.4 0.8 %fusion = bf16[64,3072]{1,0:T(8,128)(2,1)} fusion(bf16[2,64,3072]{2,1,0:T(8,128)(2,1)S(1)} %section_steps.1), kind=kLoop, calls=%fused_computation.1 | loop fusion | flops 786432 | bytes 1179648 | tf_op jit(solution)/shard_map/convert_element_type | solution.py:520
Async XLA Ops:
  0.7 1.7 %copy-start = (bf16[1,384,3072]{2,1,0:T(8,128)(2,1)S(1)}, bf16[1,384,3072]{2,1,0:T(8,128)(2,1)}, u32[]{:S(2)}) copy-start(bf16[1,384,3072]{2,1,0:T(8,128)(2,1)} %w_hbm.1) | copy-start | bytes 7077892
  2.3 1.1 %copy-start.1 = (bf16[1,1024,384]{2,1,0:T(8,128)(2,1)S(1)}, bf16[1,1024,384]{2,1,0:T(8,128)(2,1)}, u32[]{:S(2)}) copy-start(bf16[1,1024,384]{2,1,0:T(8,128)(2,1)} %k_hbm.1) | copy-start | bytes 2359300
  3.5 1.1 %copy-start.2 = (bf16[1,1024,384]{2,1,0:T(8,128)(2,1)S(1)}, bf16[1,1024,384]{2,1,0:T(8,128)(2,1)}, u32[]{:S(2)}) copy-start(bf16[1,1024,384]{2,1,0:T(8,128)(2,1)} %v_hbm.1) | copy-start | bytes 2359300
  4.6 1.0 %copy-start.3 = (bf16[64,3072]{1,0:T(8,128)(2,1)S(1)}, bf16[64,3072]{1,0:T(8,128)(2,1)}, u32[]{:S(2)}) copy-start(bf16[64,3072]{1,0:T(8,128)(2,1)} %x_hbm.1) | copy-start | bytes 1179652
  5.6 0.7 copy-start.4
  6.3 0.7 copy-start.5
  7.0 0.7 copy-start.6
  7.7 0.7 copy-start.7
  8.4 0.7 copy-start.8
  9.0 0.7 copy-start.9

commit v2 on v1

v2 whole, which is shorter than its diff:
```python
import functools
import math

import jax
import jax.numpy as jnp
from jax import lax
from jax.experimental import pallas as pl
from jax.experimental.pallas import tpu as pltpu
from jax.sharding import PartitionSpec as P

MESH = pl.DeviceIdType.MESH
BF16 = jnp.bfloat16
F32 = jnp.float32

NP = 4
EPS = 1e-06
MASKED = -1e30
HD = 128
BLK = 384
SLAB = 2 * BLK
ROWS = 64
PATCH = 256
CAP = 1024
UNIT = 32
UNITS = PATCH // UNIT
LAG = 2
TOTAL = 960
WIDTH = 3072
HALF = WIDTH // 2
EXP2_SCALE = math.log2(math.e) / math.sqrt(HD)


def mult(value, of):
    return pl.multiple_of(value, of)


def kernel(
    n_pipe,
    x_hbm,
    k_hbm,
    v_hbm,
    w_hbm,
    shift_hbm,
    scale_hbm,
    gate_hbm,
    qg_hbm,
    kg_hbm,
    lengths,
    first_patch,
    out_ref,
    xv,
    kv,
    vv,
    w4,
    shv,
    scv,
    gav,
    qgv,
    kgv,
    md,
    res,
    qb,
    fh,
    att1,
    sb1,
    rb1,
    fw1,
    xs,
    st2,
    rx,
    as2,
    att2,
    sb2,
    rb2,
    fw2,
    lsem,
    md_s,
    md_r,
    res_s,
    res_r,
    w_s,
    w_r,
    a1_s,
    a1_r,
    p1_s,
    p1_r,
    f1_s,
    f1_r,
    s2_s,
    s2_r,
    rx_s,
    rx_r,
    a2_s,
    a2_r,
    p2_s,
    p2_r,
    f2_s,
    f2_r,
):
    s = lax.axis_index("pipe")
    q = lax.axis_index("seq")
    j = q // 2
    c = q % 2
    odd = s % 2
    even = odd == 0
    pair = s + 1 - 2 * odd
    ahead = (s + 2) % n_pipe
    behind = (s + n_pipe - 2) % n_pipe
    chip = [j, 1 - j]
    slab = [2 * chip[0] + c, 2 * chip[1] + c]
    mate_slab = [2 * chip[0] + (1 - c), 2 * chip[1] + (1 - c)]
    peer = {1: mate_slab[0], 2: slab[1], 3: mate_slab[1]}
    mate = peer[1]
    own_rows = pl.ds(mult(ROWS * q, ROWS), ROWS)
    own_cols = pl.ds(mult(BLK * c, BLK), BLK)

    def block_cols(g, e):
        return pl.ds(mult(HALF * e + BLK * g, 128), BLK)

    def remote(src, dst, ssem, rsem, pipe, seq):
        return pltpu.make_async_remote_copy(
            src_ref=src,
            dst_ref=dst,
            send_sem=ssem,
            recv_sem=rsem,
            device_id={"pipe": pipe, "seq": seq},
            device_id_type=MESH,
        )

    bar = pltpu.get_barrier_semaphore()
    for k in (1, 2, 3):
        pl.semaphore_signal(bar, inc=1, device_id={"pipe": s, "seq": peer[k]}, device_id_type=MESH)
    for v in (0, 1):
        pl.semaphore_signal(bar, inc=1, device_id={"pipe": pair, "seq": slab[v]}, device_id_type=MESH)
    pl.semaphore_signal(bar, inc=1, device_id={"pipe": behind, "seq": q}, device_id_type=MESH)

    local = []

    def load(src, dst):
        copy = pltpu.make_async_copy(src, dst, lsem.at[len(local)])
        copy.start()
        local.append(copy)
        return copy

    ld_x = load(x_hbm, xv)
    ld_sc = load(scale_hbm, scv)
    ld_sh = load(shift_hbm, shv)
    ld_small = [load(gate_hbm, gav), load(qg_hbm, qgv), load(kg_hbm, kgv)]
    ld_k = load(k_hbm.at[0], kv)
    ld_v = load(v_hbm.at[0], vv)

    ld_x.wait()
    xf = xv[...].astype(F32)
    mean = jnp.sum(xf, axis=1, keepdims=True) * (1.0 / WIDTH)
    cent = xf - mean
    var = jnp.sum(cent * cent, axis=1, keepdims=True) * (1.0 / WIDTH)
    rstd = lax.rsqrt(var + EPS)
    ld_sc.wait()
    ld_sh.wait()
    md[...] = (
        (xv[:, :HALF].astype(F32) - mean) * rstd * (1.0 + scv[:, :HALF]) + shv[:, :HALF]
    ).astype(BF16)
    fh[own_rows, BLK:] = md[:, pl.ds(mult(BLK * q, 128), BLK)]

    pl.semaphore_wait(bar, 6)

    md_copies = {}
    for k in (2, 3, 1):
        md_copies[k] = remote(
            md.at[:, pl.ds(mult(BLK * peer[k], 128), BLK)],
            fh.at[own_rows, pl.ds(BLK, BLK)],
            md_s.at[k - 1],
            md_r.at[k - 1],
            s,
            peer[k],
        )
        md_copies[k].start()

    ld_res = []
    res_copies = []
    for v in (0, 1):
        for e in (0, 1):
            dst = res.at[v, pl.ds(mult(ROWS * c, ROWS), ROWS), pl.ds(BLK * e, BLK)]
            ld_res.append(load(x_hbm.at[:, block_cols(slab[v], e)], dst))
            copy = remote(
                x_hbm.at[:, block_cols(mate_slab[v], e)], dst, res_s.at[2 * v + e], res_r.at[2 * v + e], s, mate
            )
            copy.start()
            res_copies.append(copy)

    ld_w = []
    w_copies = []
    for n, (mine, his) in enumerate(
        [(slab[0], mate_slab[0]), (slab[1], mate_slab[1]), (mate_slab[0], slab[0]), (mate_slab[1], slab[1])]
    ):
        for e in (0, 1):
            for g, away in ((mine, False), (his, True)):
                src = w_hbm.at[0, :, block_cols(g, e)]
                dst = w4.at[g, own_cols, pl.ds(BLK * e, BLK)]
                if away:
                    copy = remote(src, dst, w_s.at[2 * n + e], w_r.at[2 * n + e], s, mate)
                    copy.start()
                    w_copies.append(copy)
                else:
                    ld_w.append(load(src, dst))

    for copy in ld_small:
        copy.wait()
    head_cols = pl.ds(mult(BLK * q, 128), BLK)
    scale_h = 1.0 + scv[:, head_cols]
    shift_h = shv[:, head_cols]
    q_gain = qgv[...]
    k_gain = kgv[...]

    def patch_at(t):
        p = (first_patch[0] + t + n_pipe * NP - s) % NP
        first = jnp.int32(0)
        length = jnp.int32(0)
        for n in range(NP):
            first = first + jnp.where(n < p, lengths[n], 0)
            length = length + jnp.where(n == p, lengths[n], 0)
        return first, length

    def heads(modded, rows):
        mf = modded.astype(F32)
        for h in range(BLK // HD):
            part = mf[:, HD * h : HD * (h + 1)]
            normed = part * lax.rsqrt(jnp.sum(part * part, axis=1, keepdims=True) * (1.0 / HD) + EPS)
            qb[rows, HD * h : HD * (h + 1)] = (normed * q_gain).astype(BF16)
            fh[rows, HD * h : HD * (h + 1)] = (normed * k_gain).astype(BF16)

    def refresh(first, length):
        def block(n, carry):
            rows = pl.ds(mult(n * PATCH, PATCH), PATCH)
            row = lax.broadcasted_iota(jnp.int32, (PATCH, PATCH), 0) + n * PATCH
            col = lax.broadcasted_iota(jnp.int32, (PATCH, PATCH), 1)
            pick = jnp.where((row - first == col) & (col < length), 1.0, 0.0).astype(BF16)
            placed = jnp.dot(pick, fh[...], preferred_element_type=F32)
            at = lax.broadcasted_iota(jnp.int32, (PATCH, BLK), 0) + n * PATCH
            inside = (at >= first) & (at < first + length)
            kv[rows, :] = jnp.where(inside, placed[:, :BLK], kv[rows, :].astype(F32)).astype(BF16)
            vv[rows, :] = jnp.where(inside, placed[:, BLK:], vv[rows, :].astype(F32)).astype(BF16)
            return carry

        lax.fori_loop(0, CAP // PATCH, block, 0)

    def attend(queries, live):
        parts = []
        for h in range(BLK // HD):
            cols = slice(HD * h, HD * (h + 1))
            scores = lax.dot_general(
                queries[:, cols], kv[:, cols], (((1,), (1,)), ((), ())), preferred_element_type=F32
            )
            rows = scores.shape[0]
            tail = CAP - 128
            at = lax.broadcasted_iota(jnp.int32, (rows, 128), 1) + tail
            scores = jnp.concatenate(
                [scores[:, :tail], jnp.where(at < TOTAL, scores[:, tail:], MASKED)], axis=1
            )
            top = jnp.max(scores, axis=1, keepdims=True)
            weight = jnp.exp2((scores - top) * EXP2_SCALE)
            total = jnp.sum(weight, axis=1, keepdims=True)
            out = jnp.dot(weight.astype(BF16), vv[:, cols], preferred_element_type=F32)
            parts.append(jnp.where(live, out / total, 0.0).astype(BF16))
        return jnp.concatenate(parts, axis=1)

    def gates(g):
        lo = gav[:, pl.ds(mult(BLK * g, 128), BLK)]
        hi = gav[:, pl.ds(mult(HALF + BLK * g, 128), BLK)]
        return jnp.concatenate([lo, hi], axis=1)

    first, length = patch_at(0)
    for k in (1, 2, 3):
        md_copies[k].wait_recv()

    def prep0(n, carry):
        rows = pl.ds(mult(n * ROWS, ROWS), ROWS)
        heads(fh[rows, BLK:], rows)
        return carry

    lax.fori_loop(0, PATCH // ROWS, prep0, 0)
    ld_k.wait()
    ld_v.wait()
    refresh(first, length)

    def unit_rows(i):
        return pl.ds(mult(i * UNIT, UNIT), UNIT)

    def att1_copy(i):
        part = att1.at[pl.ds(mult(i * ROWS, ROWS), ROWS), own_cols]
        return remote(part, part, a1_s.at[i], a1_r.at[i], s, mate)

    def p1_copy(i, v):
        rows = unit_rows(i)
        return remote(sb1.at[v, rows], rb1.at[v, rows], p1_s.at[v, i], p1_r.at[v, i], pair, slab[v])

    def f1_copy(i):
        rows = unit_rows(i)
        return remote(fw1.at[rows], xs.at[rows], f1_s.at[i], f1_r.at[i], ahead, q)

    for copy in ld_res:
        copy.wait()
    for copy in res_copies:
        copy.wait_recv()
    for copy in ld_w[:4]:
        copy.wait()
    for copy in w_copies[:4]:
        copy.wait_recv()

    gate1 = [gates(slab[0]), gates(slab[1])]

    def step0(i, carry):
        @pl.when(i < PATCH // ROWS)
        def _():
            rows = pl.ds(mult(i * ROWS, ROWS), ROWS)
            live = lax.broadcasted_iota(jnp.int32, (ROWS, HD), 0) + i * ROWS < length
            att1[rows, own_cols] = attend(qb[rows, :], live)
            att1_copy(i).start()

        @pl.when(i > 0)
        def _():
            n = i - 1
            att1_copy(n).wait_recv()
            rows = pl.ds(mult(n * ROWS, ROWS), ROWS)
            live = lax.broadcasted_iota(jnp.int32, (ROWS, SLAB), 0) + n * ROWS < length
            keep = live & (n // 2 == j)
            for v in (0, 1):
                proj = jnp.dot(att1[rows, :], w4[slab[v]], preferred_element_type=F32)
                held = res[v, pl.ds(mult((n % 2) * ROWS, ROWS), ROWS), :].astype(F32)
                sb1[v, rows, :] = (proj * gate1[v] + jnp.where(keep, held, 0.0)).astype(BF16)
                for u in range(ROWS // UNIT):
                    p1_copy(n * (ROWS // UNIT) + u, v).start()

        return carry

    lax.fori_loop(0, PATCH // ROWS + 1, step0, 0)

    st2[0] = jnp.zeros((UNIT, 128), F32)
    lane = lax.broadcasted_iota(jnp.int32, (UNIT, 128), 1)

    def column_stats(i):
        hf = xs[unit_rows(i), :].astype(F32)
        mean = jnp.sum(hf, axis=1, keepdims=True) * (1.0 / SLAB)
        cent = hf - mean
        spread = jnp.sum(cent * cent, axis=1, keepdims=True)
        st2[0] = jnp.where(lane == 2 * i, mean, jnp.where(lane == 2 * i + 1, spread, st2[0]))

    def take(i, carry):
        @pl.when(i < UNITS)
        def _():
            for v in (0, 1):
                p1_copy(i, v).wait_recv()
            rows = unit_rows(i)
            held = (rb1[0, rows, :].astype(F32) + rb1[1, rows, :].astype(F32)).astype(BF16)

            @pl.when(even)
            def _():
                fw1[rows, :] = held
                f1_copy(i).start()

            @pl.when(jnp.logical_not(even))
            def _():
                xs[rows, :] = held
                column_stats(i)

        @pl.when((i >= LAG) & even)
        def _():
            f1_copy(i - LAG).wait_recv()
            column_stats(i - LAG)

        return carry

    lax.fori_loop(0, UNITS + LAG, take, 0)
    s2_copies = {}
    for k in (2, 3, 1):
        s2_copies[k] = remote(st2.at[0], st2.at[k], s2_s.at[k - 1], s2_r.at[k - 1], s, peer[k])
        s2_copies[k].start()
    rx_copies = []
    for v in (0, 1):
        src = xs.at[pl.ds(mult(ROWS * mate_slab[v], ROWS), ROWS)]
        copy = remote(src, rx.at[v], rx_s.at[v], rx_r.at[v], s, mate)
        copy.start()
        rx_copies.append(copy)

    first, length = patch_at(1)
    for k in (1, 2, 3):
        s2_copies[k].wait_recv()
    stats = [st2[k] for k in range(4)]
    total = stats[0] + stats[1] + stats[2] + stats[3]
    means = total * 0.25
    spread = pltpu.roll(total, 127, 1)
    for stat in stats:
        spread = spread + (stat - means) * (stat - means) * SLAB
    rstds = lax.rsqrt(spread * (1.0 / WIDTH) + EPS)
    for i in range(UNITS):
        rows = slice(i * UNIT, (i + 1) * UNIT)
        raw = xs[rows, :BLK].astype(F32)
        mean, rstd = means[:, 2 * i : 2 * i + 1], rstds[:, 2 * i : 2 * i + 1]
        modded = ((raw - mean) * rstd * scale_h + shift_h).astype(BF16)
        fh[rows, BLK:] = modded
        heads(modded, rows)

    refresh(first, length)

    def att2_copy(i):
        rows = pl.ds(mult(i * ROWS, ROWS), ROWS)
        return remote(as2.at[rows], att2.at[rows, own_cols], a2_s.at[i], a2_r.at[i], s, mate)

    def p2_copy(u, v):
        return remote(sb2.at[v, u], rb2.at[v, u], p2_s.at[v, u], p2_r.at[v, u], pair, slab[v])

    order = [c, 1 - c, 2 + c, 3 - c]

    def f2_copy(n, p, e):
        u = n * 4 + p
        return remote(
            fw2.at[u, :, pl.ds(e * BLK, BLK)],
            out_ref.at[unit_rows(n), block_cols(order[p], e)],
            f2_s.at[e, u],
            f2_r.at[e, u],
            ahead,
            q,
        )

    for copy in rx_copies:
        copy.wait_recv()
    for copy in ld_w[4:]:
        copy.wait()
    for copy in w_copies[4:]:
        copy.wait_recv()

    bases = [ROWS * slab[0], ROWS * slab[1], ROWS * mate_slab[0], ROWS * mate_slab[1]]

    def step1(i, carry):
        @pl.when(i < 2)
        def _():
            queries = jnp.concatenate(
                [qb[pl.ds(mult(base + UNIT * i, UNIT), UNIT), :] for base in bases], axis=0
            )
            r = lax.broadcasted_iota(jnp.int32, (4 * UNIT, HD), 0)
            seg = r // UNIT
            base = jnp.where(
                seg == 0, bases[0], jnp.where(seg == 1, bases[1], jnp.where(seg == 2, bases[2], bases[3]))
            )
            live = base + UNIT * i + r % UNIT < length
            got = attend(queries, live)
            rows = pl.ds(mult(i * ROWS, ROWS), ROWS)
            att2[rows, own_cols] = got[:ROWS]
            as2[rows, :] = got[ROWS:]
            att2_copy(i).start()

        @pl.when(i > 0)
        def _():
            n = i - 1
            att2_copy(n).wait_recv()
            rows = pl.ds(mult(n * ROWS, ROWS), ROWS)
            part = unit_rows(n)
            left = att2[rows, :]
            for p, g in enumerate(order):
                proj = jnp.dot(left, w4[g], preferred_element_type=F32) * gates(g)
                if p % 2 == 0:
                    held = jnp.concatenate(
                        [xs[pl.ds(mult(base + UNIT * n, UNIT), UNIT), :] for base in bases[:2]], axis=0
                    )
                else:
                    held = jnp.concatenate([rx[0, part, :], rx[1, part, :]], axis=0)
                proj = (proj + jnp.where(p // 2 == j, held.astype(F32), 0.0)).astype(BF16)
                for v in (0, 1):
                    sb2[v, n * 4 + p] = proj[v * UNIT : (v + 1) * UNIT]
                    p2_copy(n * 4 + p, v).start()

        return carry

    lax.fori_loop(0, 3, step1, 0)

    def finish(n, carry):
        for p, g in enumerate(order):
            u = n * 4 + p
            for v in (0, 1):
                p2_copy(u, v).wait_recv()
            held = (rb2[0, u].astype(F32) + rb2[1, u].astype(F32)).astype(BF16)

            @pl.when(even)
            def _():
                fw2[u] = held
                for e in (0, 1):
                    f2_copy(n, p, e).start()

            @pl.when(jnp.logical_not(even))
            def _():
                for e in (0, 1):
                    out_ref[unit_rows(n), block_cols(g, e)] = held[:, e * BLK : (e + 1) * BLK]

        return carry

    lax.fori_loop(0, 2, finish, 0)

    @pl.when(even)
    def _():
        for i in range(UNITS):
            f1_copy(i).wait_send()
        for n in range(2):
            for p in range(4):
                for e in (0, 1):
                    f2_copy(n, p, e).wait()

    for k in (1, 2, 3):
        md_copies[k].wait_send()
        s2_copies[k].wait_send()
    for copy in res_copies + w_copies + rx_copies:
        copy.wait_send()
    for i in range(PATCH // ROWS):
        att1_copy(i).wait_send()
    for i in range(UNITS):
        for v in (0, 1):
            p1_copy(i, v).wait_send()
            p2_copy(i, v).wait_send()
    for i in range(2):
        att2_copy(i).wait_send()


def shards(n_pipe, *args):
    dma = pltpu.SemaphoreType.DMA
    vmem = pltpu.VMEM
    any_space = pl.BlockSpec(memory_space=pl.ANY)
    smem = pl.BlockSpec(memory_space=pltpu.SMEM)
    chunks = PATCH // ROWS
    return pl.pallas_call(
        functools.partial(kernel, n_pipe),
        out_shape=jax.ShapeDtypeStruct((ROWS, WIDTH), BF16),
        in_specs=[any_space] * 9 + [smem] * 2,
        out_specs=pl.BlockSpec(memory_space=vmem),
        scratch_shapes=[
            vmem((ROWS, WIDTH), BF16),
            vmem((CAP, BLK), BF16),
            vmem((CAP, BLK), BF16),
            vmem((4, SLAB, SLAB), BF16),
            vmem((1, WIDTH), F32),
            vmem((1, WIDTH), F32),
            vmem((1, WIDTH), F32),
            vmem((1, HD), F32),
            vmem((1, HD), F32),
            vmem((ROWS, HALF), BF16),
            vmem((2, 2 * ROWS, SLAB), BF16),
            vmem((PATCH, BLK), BF16),
            vmem((PATCH, SLAB), BF16),
            vmem((PATCH, SLAB), BF16),
            vmem((2, PATCH, SLAB), BF16),
            vmem((2, PATCH, SLAB), BF16),
            vmem((PATCH, SLAB), BF16),
            vmem((PATCH, SLAB), BF16),
            vmem((4, UNIT, 128), F32),
            vmem((2, ROWS, SLAB), BF16),
            vmem((2 * ROWS, BLK), BF16),
            vmem((2 * ROWS, SLAB), BF16),
            vmem((2, UNITS, UNIT, SLAB), BF16),
            vmem((2, UNITS, UNIT, SLAB), BF16),
            vmem((UNITS, UNIT, SLAB), BF16),
            dma((20,)),
            dma((3,)),
            dma((3,)),
            dma((4,)),
            dma((4,)),
            dma((8,)),
            dma((8,)),
            dma((chunks,)),
            dma((chunks,)),
            dma((2, UNITS)),
            dma((2, UNITS)),
            dma((UNITS,)),
            dma((UNITS,)),
            dma((3,)),
            dma((3,)),
            dma((2,)),
            dma((2,)),
            dma((2,)),
            dma((2,)),
            dma((2, UNITS)),
            dma((2, UNITS)),
            dma((2, UNITS)),
            dma((2, UNITS)),
        ],
        compiler_params=pltpu.CompilerParams(
            collective_id=0, has_side_effects=True, vmem_limit_bytes=60 << 20
        ),
        name="section_steps",
    )(*args)


def solution(mesh):
    in_specs = (
        P(("pipe", "seq"), None),
        P("pipe", None, "seq"),
        P("pipe", None, "seq"),
        P("pipe", "seq", None),
        P("pipe", None),
        P("pipe", None),
        P("pipe", None),
        P("pipe", None),
        P("pipe", None),
        P(),
        P(),
    )
    return jax.shard_map(
        functools.partial(shards, mesh.shape["pipe"]),
        mesh=mesh,
        in_specs=in_specs,
        out_specs=P(("pipe", "seq"), None),
        check_vma=False,
    )
```

time: 78.7 us -> 67.4 us (0.86)
  local copies, waits for them, and re-layouts: 9 us -> 1.77 us
  Pallas kernels: 67.8 us -> 64.8 us
  other arithmetic: 0.84 us -> 0 us
    unnamed x20 -> x1, local copies, waits for them, and re-layouts: 9 us -> 1.77 us
    pallas_call x1, Pallas kernels: 67.8 us -> 64.8 us  [shards(): pl.pallas_call(functools.partial(kernel, n_pipe), out_shape=jax.ShapeDtyp...]
    convert_element_type x1 -> x0, other arithmetic: 0.84 us -> none  [shards(): return (parts[0].astype(F32) + parts[1].astype(F32)).astype(BF16)]
where the time goes in v2:
time: 67.4 us; the launch traced here: 67.2 us
  Pallas kernels  64.8 us (96%)
  local copies, waits for them, and re-layouts  1.77 us (3%)
    pallas_call x1, Pallas kernels, shards(): pl.pallas_call(functools.partial(kernel, n_pipe), out_shape=jax.ShapeDtyp...  64.8 us
    unnamed x1, local copies, waits for them, and re-layouts  1.77 us

profile of v2, /device:TPU:1, one launch (start us, length us, event | category | flops | bytes accessed | tf_op | source)
XLA Modules:
  0.0 67.2 jit_solution(7942050431624701345)
XLA Ops:
  0.7 64.8 %section_steps.1 = bf16[64,3072]{1,0:T(8,128)(2,1)} custom-call(bf16[64,3072]{1,0:T(8,128)(2,1)} %x_hbm.1, bf16[1,1024,384]{2,1,0:T(8,128)(2,1)} %k_hbm.1, bf16[1,1024,384]{2,1,0:T(8,128)(2,1)} %v_hbm.1, bf16[1,384,3072]{2,1,0:T(8,128)(2,1)} %w_hbm.1, f32[1,3072]{1,0:T(1,128)} %shift_hbm.1, f32[1,3072]{1,0:T(1,128)} %scale_hbm.1, f32[1,3072]{1,0:T(1,128)} %gate_hbm.1, ...), custom_call_target="tpu_custom_call" | custom-call | tf_op jit(solution)/shard_map/section_steps/pallas_call | solution.py:528
  65.5 1.8 %copy.14 = bf16[64,3072]{1,0:T(8,128)(2,1)} copy(bf16[64,3072]{1,0:T(8,128)(2,1)} %section_steps.1) | data formatting | bytes 786432

commit v3 on v2

--- a/solution.py
+++ b/solution.py
@@ -23,7 +23,7 @@
 CAP = 1024
 UNIT = 32
 UNITS = PATCH // UNIT
-LAG = 2
+CHUNK = 128
 TOTAL = 960
 WIDTH = 3072
 HALF = WIDTH // 2
@@ -45,7 +45,7 @@
     gate_hbm,
     qg_hbm,
     kg_hbm,
-    lengths,
+    lengths_hbm,
     first_patch,
     out_ref,
     xv,
@@ -67,12 +67,15 @@
     fw1,
     xs,
     st2,
+    om,
+    ml,
     rx,
     as2,
     att2,
     sb2,
     rb2,
     fw2,
+    lengths,
     lsem,
     md_s,
     md_r,
@@ -113,6 +116,8 @@
     mate = peer[1]
     own_rows = pl.ds(mult(ROWS * q, ROWS), ROWS)
     own_cols = pl.ds(mult(BLK * c, BLK), BLK)
+    lane = lax.broadcasted_iota(jnp.int32, (ROWS, 128), 1)
+    sub = lax.broadcasted_iota(jnp.int32, (ROWS, 128), 0)
 
     def block_cols(g, e):
         return pl.ds(mult(HALF * e + BLK * g, 128), BLK)
@@ -145,7 +150,7 @@
     ld_x = load(x_hbm, xv)
     ld_sc = load(scale_hbm, scv)
     ld_sh = load(shift_hbm, shv)
-    ld_small = [load(gate_hbm, gav), load(qg_hbm, qgv), load(kg_hbm, kgv)]
+    ld_small = [load(gate_hbm, gav), load(qg_hbm, qgv), load(kg_hbm, kgv), load(lengths_hbm, lengths)]
     ld_k = load(k_hbm.at[0], kv)
     ld_v = load(v_hbm.at[0], vv)
 
@@ -244,25 +249,81 @@
 
         lax.fori_loop(0, CAP // PATCH, block, 0)
 
-    def attend(queries, live):
-        parts = []
-        for h in range(BLK // HD):
-            cols = slice(HD * h, HD * (h + 1))
-            scores = lax.dot_general(
-                queries[:, cols], kv[:, cols], (((1,), (1,)), ((), ())), preferred_element_type=F32
-            )
-            rows = scores.shape[0]
-            tail = CAP - 128
-            at = lax.broadcasted_iota(jnp.int32, (rows, 128), 1) + tail
-            scores = jnp.concatenate(
-                [scores[:, :tail], jnp.where(at < TOTAL, scores[:, tail:], MASKED)], axis=1
-            )
-            top = jnp.max(scores, axis=1, keepdims=True)
-            weight = jnp.exp2((scores - top) * EXP2_SCALE)
-            total = jnp.sum(weight, axis=1, keepdims=True)
-            out = jnp.dot(weight.astype(BF16), vv[:, cols], preferred_element_type=F32)
-            parts.append(jnp.where(live, out / total, 0.0).astype(BF16))
-        return jnp.concatenate(parts, axis=1)
+    def stale_bias(first, length):
+        at = lax.broadcasted_iota(jnp.int32, (1, CAP), 1)
+        gone = ((at >= first) & (at < first + length)) | (at >= TOTAL)
+        return jnp.where(gone, MASKED, 0.0)
+
+    def stale_scores(queries, h, bias):
+        cols = slice(HD * h, HD * (h + 1))
+        return bias + lax.dot_general(
+            queries[:, cols], kv[:, cols], (((1,), (1,)), ((), ())), preferred_element_type=F32
+        )
+
+    def fresh_scores(queries, h, length):
+        cols = slice(HD * h, HD * (h + 1))
+        scores = lax.dot_general(
+            queries[:, cols], fh[:, cols], (((1,), (1,)), ((), ())), preferred_element_type=F32
+        )
+        at = lax.broadcasted_iota(jnp.int32, scores.shape, 1)
+        return jnp.where(at < length, scores, MASKED)
+
+    def weigh(scores, top):
+        weight = jnp.exp2((scores - top) * EXP2_SCALE)
+        return weight.astype(BF16), jnp.sum(weight, axis=1, keepdims=True)
+
+    def stale_values(weight, h):
+        return jnp.dot(weight, vv[:, HD * h : HD * (h + 1)], preferred_element_type=F32)
+
+    def fresh_values(weight, h):
+        cols = slice(BLK + HD * h, BLK + HD * (h + 1))
+        return jnp.dot(weight, fh[:, cols], preferred_element_type=F32)
+
+    heads_here = range(BLK // HD)
+
+    def tops(scores):
+        return [jnp.max(part, axis=1, keepdims=True) for part in scores]
+
+    def attend(queries, live, bias, length):
+        old = [stale_scores(queries, h, bias) for h in heads_here]
+        new = [fresh_scores(queries, h, length) for h in heads_here]
+        top = [jnp.maximum(a, b) for a, b in zip(tops(old), tops(new))]
+        old = [weigh(part, m) for part, m in zip(old, top)]
+        new = [weigh(part, m) for part, m in zip(new, top)]
+        out = [stale_values(old[h][0], h) + fresh_values(new[h][0], h) for h in heads_here]
+        return jnp.concatenate(
+            [jnp.where(live, out[h] / (old[h][1] + new[h][1]), 0.0).astype(BF16) for h in heads_here], axis=1
+        )
+
+    def attend_stale(rows, bias):
+        queries = qb[rows, :]
+        scores = [stale_scores(queries, h, bias) for h in heads_here]
+        top = tops(scores)
+        old = [weigh(part, m) for part, m in zip(scores, top)]
+        out = [stale_values(old[h][0], h) for h in heads_here]
+        tile = jnp.zeros((ROWS, 128), F32)
+        for h in heads_here:
+            tile = jnp.where(lane == h, top[h], jnp.where(lane == 8 + h, old[h][1], tile))
+        om[rows, :] = jnp.concatenate(out, axis=1)
+        ml[rows, :] = tile
+
+    def attend_fresh(queries, out, tile, live, length):
+        scores = [fresh_scores(queries, h, length) for h in heads_here]
+        old_top = [tile[:, h : h + 1] for h in heads_here]
+        old_total = [tile[:, 8 + h : 9 + h] for h in heads_here]
+        top = [jnp.maximum(a, b) for a, b in zip(old_top, tops(scores))]
+        new = [weigh(part, m) for part, m in zip(scores, top)]
+        shrink = [jnp.exp2((a - b) * EXP2_SCALE) for a, b in zip(old_top, top)]
+        got = [
+            out[:, HD * h : HD * (h + 1)] * shrink[h] + fresh_values(new[h][0], h) for h in heads_here
+        ]
+        return jnp.concatenate(
+            [
+                jnp.where(live, got[h] / (old_total[h] * shrink[h] + new[h][1]), 0.0).astype(BF16)
+                for h in heads_here
+            ],
+            axis=1,
+        )
 
     def gates(g):
         lo = gav[:, pl.ds(mult(BLK * g, 128), BLK)]
@@ -281,13 +342,15 @@
     lax.fori_loop(0, PATCH // ROWS, prep0, 0)
     ld_k.wait()
     ld_v.wait()
-    refresh(first, length)
+    bias = stale_bias(first, length)
+    next_first, next_length = patch_at(1)
+    next_bias = stale_bias(next_first, next_length)
 
     def unit_rows(i):
         return pl.ds(mult(i * UNIT, UNIT), UNIT)
 
     def att1_copy(i):
-        part = att1.at[pl.ds(mult(i * ROWS, ROWS), ROWS), own_cols]
+        part = att1.at[pl.ds(mult(i * CHUNK, CHUNK), CHUNK), own_cols]
         return remote(part, part, a1_s.at[i], a1_r.at[i], s, mate)
 
     def p1_copy(i, v):
@@ -309,45 +372,52 @@
 
     gate1 = [gates(slab[0]), gates(slab[1])]
 
-    def step0(i, carry):
-        @pl.when(i < PATCH // ROWS)
-        def _():
-            rows = pl.ds(mult(i * ROWS, ROWS), ROWS)
-            live = lax.broadcasted_iota(jnp.int32, (ROWS, HD), 0) + i * ROWS < length
-            att1[rows, own_cols] = attend(qb[rows, :], live)
-            att1_copy(i).start()
-
-        @pl.when(i > 0)
-        def _():
-            n = i - 1
-            att1_copy(n).wait_recv()
-            rows = pl.ds(mult(n * ROWS, ROWS), ROWS)
-            live = lax.broadcasted_iota(jnp.int32, (ROWS, SLAB), 0) + n * ROWS < length
-            keep = live & (n // 2 == j)
-            for v in (0, 1):
-                proj = jnp.dot(att1[rows, :], w4[slab[v]], preferred_element_type=F32)
-                held = res[v, pl.ds(mult((n % 2) * ROWS, ROWS), ROWS), :].astype(F32)
-                sb1[v, rows, :] = (proj * gate1[v] + jnp.where(keep, held, 0.0)).astype(BF16)
-                for u in range(ROWS // UNIT):
-                    p1_copy(n * (ROWS // UNIT) + u, v).start()
-
-        return carry
-
-    lax.fori_loop(0, PATCH // ROWS + 1, step0, 0)
-
-    st2[0] = jnp.zeros((UNIT, 128), F32)
-    lane = lax.broadcasted_iota(jnp.int32, (UNIT, 128), 1)
-
-    def column_stats(i):
-        hf = xs[unit_rows(i), :].astype(F32)
+    def s2_copy(g, k):
+        return remote(st2.at[0, g], st2.at[k, g], s2_s.at[k - 1, g], s2_r.at[k - 1, g], s, peer[k])
+
+    def rx_copy(g):
+        v = jnp.where(g // 2 == j, 0, 1)
+        src = xs.at[pl.ds(mult(g * ROWS, ROWS), ROWS)]
+        return remote(src, rx.at[v], rx_s.at[v], rx_r.at[v], s, mate)
+
+    def ready(g):
+        hf = xs[pl.ds(mult(g * ROWS, ROWS), ROWS), :].astype(F32)
         mean = jnp.sum(hf, axis=1, keepdims=True) * (1.0 / SLAB)
         cent = hf - mean
         spread = jnp.sum(cent * cent, axis=1, keepdims=True)
-        st2[0] = jnp.where(lane == 2 * i, mean, jnp.where(lane == 2 * i + 1, spread, st2[0]))
-
-    def take(i, carry):
-        @pl.when(i < UNITS)
+        tile = jnp.where(lane == sub, mean, jnp.where(lane == sub + ROWS, spread, 0.0))
+        st2[0, g] = jnp.sum(tile, axis=0, keepdims=True)
+        for k in (2, 3, 1):
+            s2_copy(g, k).start()
+
+        @pl.when(g % 2 != c)
         def _():
+            rx_copy(g).start()
+
+    def process(g):
+        for k in (1, 2, 3):
+            s2_copy(g, k).wait_recv()
+        stats = [st2[k, g] for k in range(4)]
+        total = stats[0] + stats[1] + stats[2] + stats[3]
+        means = total * 0.25
+        apart = jnp.zeros((1, 128), F32)
+        for stat in stats:
+            apart = apart + (stat - means) * (stat - means) * SLAB
+        both = jnp.where(lane[:1] < ROWS, apart, total)
+        mean = jnp.sum(jnp.where(lane == sub, means, 0.0), axis=1, keepdims=True)
+        spread = jnp.sum(
+            jnp.where((lane == sub) | (lane == sub + ROWS), both, 0.0), axis=1, keepdims=True
+        )
+        rstd = lax.rsqrt(spread * (1.0 / WIDTH) + EPS)
+        rows = pl.ds(mult(g * ROWS, ROWS), ROWS)
+        modded = ((xs[rows, :BLK].astype(F32) - mean) * rstd * scale_h + shift_h).astype(BF16)
+        fh[rows, BLK:] = modded
+        heads(modded, rows)
+        attend_stale(rows, next_bias)
+
+    def take(g):
+        for u in range(ROWS // UNIT):
+            i = g * (ROWS // UNIT) + u
             for v in (0, 1):
                 p1_copy(i, v).wait_recv()
             rows = unit_rows(i)
@@ -361,46 +431,57 @@
             @pl.when(jnp.logical_not(even))
             def _():
                 xs[rows, :] = held
-                column_stats(i)
-
-        @pl.when((i >= LAG) & even)
+
+    def taken(g):
+        for u in range(ROWS // UNIT):
+            f1_copy(g * (ROWS // UNIT) + u).wait_recv()
+
+    groups = PATCH // ROWS
+
+    def step0(i, carry):
+        rows = pl.ds(mult(i * CHUNK, CHUNK), CHUNK)
+        live = lax.broadcasted_iota(jnp.int32, (CHUNK, HD), 0) + i * CHUNK < length
+        att1[rows, own_cols] = attend(qb[rows, :], live, bias, length)
+        att1_copy(i).start()
+        att1_copy(i).wait_recv()
+        live = lax.broadcasted_iota(jnp.int32, (CHUNK, SLAB), 0) + i * CHUNK < length
+        keep = live & (i == j)
+        for v in (0, 1):
+            proj = jnp.dot(att1[rows, :], w4[slab[v]], preferred_element_type=F32)
+            held = res[v].astype(F32)
+            sb1[v, rows, :] = (proj * gate1[v] + jnp.where(keep, held, 0.0)).astype(BF16)
+            for u in range(CHUNK // UNIT):
+                p1_copy(i * (CHUNK // UNIT) + u, v).start()
+        return carry
+
+    lax.fori_loop(0, PATCH // CHUNK, step0, 0)
+    refresh(first, length)
+
+    def hand_over(i, carry):
+        @pl.when(i < groups)
         def _():
-            f1_copy(i - LAG).wait_recv()
-            column_stats(i - LAG)
+            take(i)
+
+        @pl.when((i < groups) & jnp.logical_not(even))
+        def _():
+            ready(i)
+
+        @pl.when((i >= 1) & (i < 1 + groups) & even)
+        def _():
+            taken(i - 1)
+            ready(i - 1)
+
+        done = i - 1 - (1 - odd)
+
+        @pl.when((done >= 0) & (done < groups))
+        def _():
+            process(done)
 
         return carry
 
-    lax.fori_loop(0, UNITS + LAG, take, 0)
-    s2_copies = {}
-    for k in (2, 3, 1):
-        s2_copies[k] = remote(st2.at[0], st2.at[k], s2_s.at[k - 1], s2_r.at[k - 1], s, peer[k])
-        s2_copies[k].start()
-    rx_copies = []
-    for v in (0, 1):
-        src = xs.at[pl.ds(mult(ROWS * mate_slab[v], ROWS), ROWS)]
-        copy = remote(src, rx.at[v], rx_s.at[v], rx_r.at[v], s, mate)
-        copy.start()
-        rx_copies.append(copy)
-
-    first, length = patch_at(1)
-    for k in (1, 2, 3):
-        s2_copies[k].wait_recv()
-    stats = [st2[k] for k in range(4)]
-    total = stats[0] + stats[1] + stats[2] + stats[3]
-    means = total * 0.25
-    spread = pltpu.roll(total, 127, 1)
-    for stat in stats:
-        spread = spread + (stat - means) * (stat - means) * SLAB
-    rstds = lax.rsqrt(spread * (1.0 / WIDTH) + EPS)
-    for i in range(UNITS):
-        rows = slice(i * UNIT, (i + 1) * UNIT)
-        raw = xs[rows, :BLK].astype(F32)
-        mean, rstd = means[:, 2 * i : 2 * i + 1], rstds[:, 2 * i : 2 * i + 1]
-        modded = ((raw - mean) * rstd * scale_h + shift_h).astype(BF16)
-        fh[rows, BLK:] = modded
-        heads(modded, rows)
-
-    refresh(first, length)
+    lax.fori_loop(0, groups + 2, hand_over, 0)
+
+    first, length = next_first, next_length
 
     def att2_copy(i):
         rows = pl.ds(mult(i * ROWS, ROWS), ROWS)
@@ -422,14 +503,32 @@
             q,
         )
 
-    for copy in rx_copies:
-        copy.wait_recv()
+    for v in (0, 1):
+        rx_copy(mate_slab[v]).wait_recv()
     for copy in ld_w[4:]:
         copy.wait()
     for copy in w_copies[4:]:
         copy.wait_recv()
 
     bases = [ROWS * slab[0], ROWS * slab[1], ROWS * mate_slab[0], ROWS * mate_slab[1]]
+
+    def finish(n):
+        for p, g in enumerate(order):
+            u = n * 4 + p
+            for v in (0, 1):
+                p2_copy(u, v).wait_recv()
+            held = (rb2[0, u].astype(F32) + rb2[1, u].astype(F32)).astype(BF16)
+
+            @pl.when(even)
+            def _():
+                fw2[u] = held
+                for e in (0, 1):
+                    f2_copy(n, p, e).start()
+
+            @pl.when(jnp.logical_not(even))
+            def _():
+                for e in (0, 1):
+                    out_ref[unit_rows(n), block_cols(g, e)] = held[:, e * BLK : (e + 1) * BLK]
 
     def step1(i, carry):
         @pl.when(i < 2)
@@ -443,13 +542,16 @@
                 seg == 0, bases[0], jnp.where(seg == 1, bases[1], jnp.where(seg == 2, bases[2], bases[3]))
             )
             live = base + UNIT * i + r % UNIT < length
-            got = attend(queries, live)
+            seen = [pl.ds(mult(base + UNIT * i, UNIT), UNIT) for base in bases]
+            out = jnp.concatenate([om[part, :] for part in seen], axis=0)
+            tile = jnp.concatenate([ml[part, :] for part in seen], axis=0)
+            got = attend_fresh(queries, out, tile, live, length)
             rows = pl.ds(mult(i * ROWS, ROWS), ROWS)
             att2[rows, own_cols] = got[:ROWS]
             as2[rows, :] = got[ROWS:]
             att2_copy(i).start()
 
-        @pl.when(i > 0)
+        @pl.when((i > 0) & (i < 3))
         def _():
             n = i - 1
             att2_copy(n).wait_recv()
@@ -469,31 +571,13 @@
                     sb2[v, n * 4 + p] = proj[v * UNIT : (v + 1) * UNIT]
                     p2_copy(n * 4 + p, v).start()
 
+        @pl.when(i > 1)
+        def _():
+            finish(i - 2)
+
         return carry
 
-    lax.fori_loop(0, 3, step1, 0)
-
-    def finish(n, carry):
-        for p, g in enumerate(order):
-            u = n * 4 + p
-            for v in (0, 1):
-                p2_copy(u, v).wait_recv()
-            held = (rb2[0, u].astype(F32) + rb2[1, u].astype(F32)).astype(BF16)
-
-            @pl.when(even)
-            def _():
-                fw2[u] = held
-                for e in (0, 1):
-                    f2_copy(n, p, e).start()
-
-            @pl.when(jnp.logical_not(even))
-            def _():
-                for e in (0, 1):
-                    out_ref[unit_rows(n), block_cols(g, e)] = held[:, e * BLK : (e + 1) * BLK]
-
-        return carry
-
-    lax.fori_loop(0, 2, finish, 0)
+    lax.fori_loop(0, 4, step1, 0)
 
     @pl.when(even)
     def _():
@@ -506,10 +590,13 @@
 
     for k in (1, 2, 3):
         md_copies[k].wait_send()
-        s2_copies[k].wait_send()
-    for copy in res_copies + w_copies + rx_copies:
+        for g in range(groups):
+            s2_copy(g, k).wait_send()
+    for v in (0, 1):
+        rx_copy(mate_slab[v]).wait_send()
+    for copy in res_copies + w_copies:
         copy.wait_send()
-    for i in range(PATCH // ROWS):
+    for i in range(PATCH // CHUNK):
         att1_copy(i).wait_send()
     for i in range(UNITS):
         for v in (0, 1):
@@ -525,10 +612,11 @@
     any_space = pl.BlockSpec(memory_space=pl.ANY)
     smem = pl.BlockSpec(memory_space=pltpu.SMEM)
     chunks = PATCH // ROWS
+    held = [pltpu.with_memory_space_constraint(arg, pltpu.HBM) for arg in args[:10]]
     return pl.pallas_call(
         functools.partial(kernel, n_pipe),
         out_shape=jax.ShapeDtypeStruct((ROWS, WIDTH), BF16),
-        in_specs=[any_space] * 9 + [smem] * 2,
+        in_specs=[any_space] * 10 + [smem],
         out_specs=pl.BlockSpec(memory_space=vmem),
         scratch_shapes=[
             vmem((ROWS, WIDTH), BF16),
@@ -549,28 +637,31 @@
             vmem((2, PATCH, SLAB), BF16),
             vmem((PATCH, SLAB), BF16),
             vmem((PATCH, SLAB), BF16),
-            vmem((4, UNIT, 128), F32),
+            vmem((4, chunks, 1, 128), F32),
+            vmem((PATCH, BLK), F32),
+            vmem((PATCH, 128), F32),
             vmem((2, ROWS, SLAB), BF16),
             vmem((2 * ROWS, BLK), BF16),
             vmem((2 * ROWS, SLAB), BF16),
             vmem((2, UNITS, UNIT, SLAB), BF16),
             vmem((2, UNITS, UNIT, SLAB), BF16),
             vmem((UNITS, UNIT, SLAB), BF16),
-            dma((20,)),
+            pltpu.SMEM((NP,), jnp.int32),
+            dma((21,)),
             dma((3,)),
             dma((3,)),
             dma((4,)),
             dma((4,)),
             dma((8,)),
             dma((8,)),
-            dma((chunks,)),
-            dma((chunks,)),
+            dma((PATCH // CHUNK,)),
+            dma((PATCH // CHUNK,)),
             dma((2, UNITS)),
             dma((2, UNITS)),
             dma((UNITS,)),
             dma((UNITS,)),
-            dma((3,)),
-            dma((3,)),
+            dma((3, chunks)),
+            dma((3, chunks)),
             dma((2,)),
             dma((2,)),
             dma((2,)),
@@ -581,10 +672,10 @@
             dma((2, UNITS)),
         ],
         compiler_params=pltpu.CompilerParams(
-            collective_id=0, has_side_effects=True, vmem_limit_bytes=60 << 20
+            collective_id=0, has_side_effects=True, vmem_limit_bytes=40 << 20
         ),
         name="section_steps",
-    )(*args)
+    )(*held, args[10])
 
 
 def solution(mesh):

time: 67.4 us -> 63 us (0.935)
  Pallas kernels: 64.8 us -> 61.4 us
  local copies, waits for them, and re-layouts: 1.77 us -> 0.75 us
    pallas_call x1, Pallas kernels: 64.8 us -> 61.4 us  [shards(): pl.pallas_call(functools.partial(kernel, n_pipe), out_shape=jax.ShapeDtyp...]
    unnamed x1, local copies, waits for them, and re-layouts: 1.77 us -> 0.75 us
where the time goes in v3:
time: 63 us; the launch traced here: 62.8 us
  Pallas kernels  61.4 us (97%)
  local copies, waits for them, and re-layouts  0.75 us (1%)
  between operations  0.66 us (1%)
    pallas_call x1, Pallas kernels, shards(): pl.pallas_call(functools.partial(kernel, n_pipe), out_shape=jax.ShapeDtyp...  61.4 us

profile of v3, /device:TPU:1, one launch (start us, length us, event | category | flops | bytes accessed | tf_op | source)
XLA Modules:
  0.0 62.8 jit_solution(2970004045839834988)
XLA Ops:
  0.7 61.4 %section_steps.1 = bf16[64,3072]{1,0:T(8,128)(2,1)S(1)} custom-call(bf16[64,3072]{1,0:T(8,128)(2,1)} %x_hbm.1, bf16[1,1024,384]{2,1,0:T(8,128)(2,1)} %k_hbm.1, bf16[1,1024,384]{2,1,0:T(8,128)(2,1)} %v_hbm.1, bf16[1,384,3072]{2,1,0:T(8,128)(2,1)} %w_hbm.1, f32[1,3072]{1,0:T(1,128)} %shift_hbm.1, f32[1,3072]{1,0:T(1,128)} %scale_hbm.1, f32[1,3072]{1,0:T(1,128)} %gate_hbm.1, ...), custom_call_target="tpu_custom_call" | custom-call | tf_op jit(solution)/shard_map/section_steps/pallas_call | solution.py:616
  62.1 0.7 %copy.14 = bf16[64,3072]{1,0:T(8,128)(2,1)} copy(bf16[64,3072]{1,0:T(8,128)(2,1)S(1)} %section_steps.1) | data formatting | bytes 786432

commit v4 on v3

--- a/solution.py
+++ b/solution.py
@@ -23,6 +23,9 @@
 CAP = 1024
 UNIT = 32
 UNITS = PATCH // UNIT
+UNIT1 = 32
+UNITS1 = PATCH // UNIT1
+BEHIND = 2
 CHUNK = 128
 TOTAL = 960
 WIDTH = 3072
@@ -167,6 +170,23 @@
     ).astype(BF16)
     fh[own_rows, BLK:] = md[:, pl.ds(mult(BLK * q, 128), BLK)]
 
+    for copy in ld_small:
+        copy.wait()
+    head_cols = pl.ds(mult(BLK * q, 128), BLK)
+    scale_h = 1.0 + scv[:, head_cols]
+    shift_h = shv[:, head_cols]
+    q_gain = qgv[...]
+    k_gain = kgv[...]
+
+    def heads(modded, rows):
+        mf = modded.astype(F32)
+        for h in range(BLK // HD):
+            part = mf[:, HD * h : HD * (h + 1)]
+            normed = part * lax.rsqrt(jnp.sum(part * part, axis=1, keepdims=True) * (1.0 / HD) + EPS)
+            qb[rows, HD * h : HD * (h + 1)] = (normed * q_gain).astype(BF16)
+            fh[rows, HD * h : HD * (h + 1)] = (normed * k_gain).astype(BF16)
+
+    heads(fh[own_rows, BLK:], own_rows)
     pl.semaphore_wait(bar, 6)
 
     md_copies = {}
@@ -209,14 +229,6 @@
                 else:
                     ld_w.append(load(src, dst))
 
-    for copy in ld_small:
-        copy.wait()
-    head_cols = pl.ds(mult(BLK * q, 128), BLK)
-    scale_h = 1.0 + scv[:, head_cols]
-    shift_h = shv[:, head_cols]
-    q_gain = qgv[...]
-    k_gain = kgv[...]
-
     def patch_at(t):
         p = (first_patch[0] + t + n_pipe * NP - s) % NP
         first = jnp.int32(0)
@@ -225,14 +237,6 @@
             first = first + jnp.where(n < p, lengths[n], 0)
             length = length + jnp.where(n == p, lengths[n], 0)
         return first, length
-
-    def heads(modded, rows):
-        mf = modded.astype(F32)
-        for h in range(BLK // HD):
-            part = mf[:, HD * h : HD * (h + 1)]
-            normed = part * lax.rsqrt(jnp.sum(part * part, axis=1, keepdims=True) * (1.0 / HD) + EPS)
-            qb[rows, HD * h : HD * (h + 1)] = (normed * q_gain).astype(BF16)
-            fh[rows, HD * h : HD * (h + 1)] = (normed * k_gain).astype(BF16)
 
     def refresh(first, length):
         def block(n, carry):
@@ -295,35 +299,32 @@
             [jnp.where(live, out[h] / (old[h][1] + new[h][1]), 0.0).astype(BF16) for h in heads_here], axis=1
         )
 
+    def soften(scores, values):
+        top = tops(scores)
+        weight = [weigh(part, m) for part, m in zip(scores, top)]
+        return top, [part[1] for part in weight], [values(weight[h][0], h) for h in heads_here]
+
+    def keep_stale(rows, top, total, out):
+        tile = jnp.zeros((ROWS, 128), F32)
+        for h in heads_here:
+            tile = jnp.where(lane == h, top[h], jnp.where(lane == 8 + h, total[h], tile))
+        om[rows, :] = jnp.concatenate(out, axis=1)
+        ml[rows, :] = tile
+
     def attend_stale(rows, bias):
         queries = qb[rows, :]
-        scores = [stale_scores(queries, h, bias) for h in heads_here]
-        top = tops(scores)
-        old = [weigh(part, m) for part, m in zip(scores, top)]
-        out = [stale_values(old[h][0], h) for h in heads_here]
-        tile = jnp.zeros((ROWS, 128), F32)
-        for h in heads_here:
-            tile = jnp.where(lane == h, top[h], jnp.where(lane == 8 + h, old[h][1], tile))
-        om[rows, :] = jnp.concatenate(out, axis=1)
-        ml[rows, :] = tile
-
-    def attend_fresh(queries, out, tile, live, length):
-        scores = [fresh_scores(queries, h, length) for h in heads_here]
-        old_top = [tile[:, h : h + 1] for h in heads_here]
-        old_total = [tile[:, 8 + h : 9 + h] for h in heads_here]
-        top = [jnp.maximum(a, b) for a, b in zip(old_top, tops(scores))]
-        new = [weigh(part, m) for part, m in zip(scores, top)]
-        shrink = [jnp.exp2((a - b) * EXP2_SCALE) for a, b in zip(old_top, top)]
-        got = [
-            out[:, HD * h : HD * (h + 1)] * shrink[h] + fresh_values(new[h][0], h) for h in heads_here
-        ]
-        return jnp.concatenate(
-            [
-                jnp.where(live, got[h] / (old_total[h] * shrink[h] + new[h][1]), 0.0).astype(BF16)
-                for h in heads_here
-            ],
-            axis=1,
-        )
+        keep_stale(rows, *soften([stale_scores(queries, h, bias) for h in heads_here], stale_values))
+
+    def merge_parts(out, tile, fresh, live):
+        parts = []
+        for h, (top, total, got) in enumerate(zip(*fresh)):
+            old_top, old_total = tile[:, h : h + 1], tile[:, 8 + h : 9 + h]
+            both = jnp.maximum(old_top, top)
+            a = jnp.exp2((old_top - both) * EXP2_SCALE)
+            b = jnp.exp2((top - both) * EXP2_SCALE)
+            got = out[:, HD * h : HD * (h + 1)] * a + got * b
+            parts.append(jnp.where(live, got / (old_total * a + total * b), 0.0).astype(BF16))
+        return jnp.concatenate(parts, axis=1)
 
     def gates(g):
         lo = gav[:, pl.ds(mult(BLK * g, 128), BLK)]
@@ -333,13 +334,8 @@
     first, length = patch_at(0)
     for k in (1, 2, 3):
         md_copies[k].wait_recv()
-
-    def prep0(n, carry):
-        rows = pl.ds(mult(n * ROWS, ROWS), ROWS)
+        rows = pl.ds(mult(ROWS * peer[k], ROWS), ROWS)
         heads(fh[rows, BLK:], rows)
-        return carry
-
-    lax.fori_loop(0, PATCH // ROWS, prep0, 0)
     ld_k.wait()
     ld_v.wait()
     bias = stale_bias(first, length)
@@ -349,16 +345,19 @@
     def unit_rows(i):
         return pl.ds(mult(i * UNIT, UNIT), UNIT)
 
+    def unit1_rows(i):
+        return pl.ds(mult(i * UNIT1, UNIT1), UNIT1)
+
     def att1_copy(i):
         part = att1.at[pl.ds(mult(i * CHUNK, CHUNK), CHUNK), own_cols]
         return remote(part, part, a1_s.at[i], a1_r.at[i], s, mate)
 
     def p1_copy(i, v):
-        rows = unit_rows(i)
+        rows = unit1_rows(i)
         return remote(sb1.at[v, rows], rb1.at[v, rows], p1_s.at[v, i], p1_r.at[v, i], pair, slab[v])
 
     def f1_copy(i):
-        rows = unit_rows(i)
+        rows = unit1_rows(i)
         return remote(fw1.at[rows], xs.at[rows], f1_s.at[i], f1_r.at[i], ahead, q)
 
     for copy in ld_res:
@@ -413,14 +412,17 @@
         modded = ((xs[rows, :BLK].astype(F32) - mean) * rstd * scale_h + shift_h).astype(BF16)
         fh[rows, BLK:] = modded
         heads(modded, rows)
-        attend_stale(rows, next_bias)
+
+        @pl.when(g < groups - 1)
+        def _():
+            attend_stale(rows, next_bias)
 
     def take(g):
-        for u in range(ROWS // UNIT):
-            i = g * (ROWS // UNIT) + u
+        for u in range(ROWS // UNIT1):
+            i = g * (ROWS // UNIT1) + u
             for v in (0, 1):
                 p1_copy(i, v).wait_recv()
-            rows = unit_rows(i)
+            rows = unit1_rows(i)
             held = (rb1[0, rows, :].astype(F32) + rb1[1, rows, :].astype(F32)).astype(BF16)
 
             @pl.when(even)
@@ -433,8 +435,8 @@
                 xs[rows, :] = held
 
     def taken(g):
-        for u in range(ROWS // UNIT):
-            f1_copy(g * (ROWS // UNIT) + u).wait_recv()
+        for u in range(ROWS // UNIT1):
+            f1_copy(g * (ROWS // UNIT1) + u).wait_recv()
 
     groups = PATCH // ROWS
 
@@ -450,8 +452,8 @@
             proj = jnp.dot(att1[rows, :], w4[slab[v]], preferred_element_type=F32)
             held = res[v].astype(F32)
             sb1[v, rows, :] = (proj * gate1[v] + jnp.where(keep, held, 0.0)).astype(BF16)
-            for u in range(CHUNK // UNIT):
-                p1_copy(i * (CHUNK // UNIT) + u, v).start()
+            for u in range(CHUNK // UNIT1):
+                p1_copy(i * (CHUNK // UNIT1) + u, v).start()
         return carry
 
     lax.fori_loop(0, PATCH // CHUNK, step0, 0)
@@ -487,21 +489,16 @@
         rows = pl.ds(mult(i * ROWS, ROWS), ROWS)
         return remote(as2.at[rows], att2.at[rows, own_cols], a2_s.at[i], a2_r.at[i], s, mate)
 
-    def p2_copy(u, v):
-        return remote(sb2.at[v, u], rb2.at[v, u], p2_s.at[v, u], p2_r.at[v, u], pair, slab[v])
-
-    order = [c, 1 - c, 2 + c, 3 - c]
-
-    def f2_copy(n, p, e):
-        u = n * 4 + p
-        return remote(
-            fw2.at[u, :, pl.ds(e * BLK, BLK)],
-            out_ref.at[unit_rows(n), block_cols(order[p], e)],
-            f2_s.at[e, u],
-            f2_r.at[e, u],
-            ahead,
-            q,
-        )
+    def slab_of(u):
+        p = u % 4
+        return 2 * (p // 2) + (c + p % 2) % 2
+
+    def p2_copy(u, e, v):
+        return remote(sb2.at[v, u, e], rb2.at[v, u, e], p2_s.at[v, u, e], p2_r.at[v, u, e], pair, slab[v])
+
+    def f2_copy(u, e):
+        dst = out_ref.at[unit_rows(u // 4), block_cols(slab_of(u), e)]
+        return remote(fw2.at[u, e], dst, f2_s.at[u, e], f2_r.at[u, e], ahead, q)
 
     for v in (0, 1):
         rx_copy(mate_slab[v]).wait_recv()
@@ -512,81 +509,103 @@
 
     bases = [ROWS * slab[0], ROWS * slab[1], ROWS * mate_slab[0], ROWS * mate_slab[1]]
 
-    def finish(n):
-        for p, g in enumerate(order):
-            u = n * 4 + p
+    def finish(u):
+        for e in (0, 1):
             for v in (0, 1):
-                p2_copy(u, v).wait_recv()
-            held = (rb2[0, u].astype(F32) + rb2[1, u].astype(F32)).astype(BF16)
+                p2_copy(u, e, v).wait_recv()
+            held = (rb2[0, u, e].astype(F32) + rb2[1, u, e].astype(F32)).astype(BF16)
 
             @pl.when(even)
             def _():
-                fw2[u] = held
-                for e in (0, 1):
-                    f2_copy(n, p, e).start()
+                fw2[u, e] = held
+                f2_copy(u, e).start()
 
             @pl.when(jnp.logical_not(even))
             def _():
+                out_ref[unit_rows(u // 4), block_cols(slab_of(u), e)] = held
+
+    r = lax.broadcasted_iota(jnp.int32, (4 * UNIT, HD), 0)
+    seg = r // UNIT
+    start = jnp.where(
+        seg == 0, bases[0], jnp.where(seg == 1, bases[1], jnp.where(seg == 2, bases[2], bases[3]))
+    )
+
+    def merge(i, last=None):
+        seen = [pl.ds(mult(base + UNIT * i, UNIT), UNIT) for base in bases]
+        queries = jnp.concatenate([qb[part, :] for part in seen], axis=0)
+        new = [fresh_scores(queries, h, length) for h in heads_here]
+        if last is None:
+            fresh = soften(new, fresh_values)
+        else:
+            late = qb[last, :]
+            old = [stale_scores(late, h, next_bias) for h in heads_here]
+            old_top, new_top = tops(old), tops(new)
+            old = [weigh(part, m) for part, m in zip(old, old_top)]
+            new = [weigh(part, m) for part, m in zip(new, new_top)]
+            old_out = [stale_values(old[h][0], h) for h in heads_here]
+            fresh = new_top, [part[1] for part in new], [fresh_values(new[h][0], h) for h in heads_here]
+            keep_stale(last, old_top, [part[1] for part in old], old_out)
+        out = jnp.concatenate([om[part, :] for part in seen], axis=0)
+        tile = jnp.concatenate([ml[part, :] for part in seen], axis=0)
+        live = start + UNIT * i + r % UNIT < length
+        got = merge_parts(out, tile, fresh, live)
+        rows = pl.ds(i * ROWS, ROWS)
+        att2[rows, own_cols] = got[:ROWS]
+        as2[rows, :] = got[ROWS:]
+        att2_copy(i).start()
+
+    merge(0, pl.ds(PATCH - ROWS, ROWS))
+    merge(1)
+
+    def step1(u, carry):
+        n = u // 4
+        p = u % 4
+
+        @pl.when(p == 0)
+        def _():
+            att2_copy(n).wait_recv()
+
+        @pl.when(u < UNITS)
+        def _():
+            g = slab_of(u)
+            part = unit_rows(n)
+            left = att2[pl.ds(mult(n * ROWS, ROWS), ROWS), :]
+            proj = jnp.dot(left, w4[g], preferred_element_type=F32) * gates(g)
+            own = jnp.concatenate(
+                [xs[pl.ds(mult(base + UNIT * n, UNIT), UNIT), :] for base in bases[:2]], axis=0
+            )
+            his = jnp.concatenate([rx[0, part, :], rx[1, part, :]], axis=0)
+            held = jnp.where(p % 2 == 0, own.astype(F32), his.astype(F32))
+            proj = (proj + jnp.where(p // 2 == j, held, 0.0)).astype(BF16)
+            for v in (0, 1):
                 for e in (0, 1):
-                    out_ref[unit_rows(n), block_cols(g, e)] = held[:, e * BLK : (e + 1) * BLK]
-
-    def step1(i, carry):
-        @pl.when(i < 2)
-        def _():
-            queries = jnp.concatenate(
-                [qb[pl.ds(mult(base + UNIT * i, UNIT), UNIT), :] for base in bases], axis=0
-            )
-            r = lax.broadcasted_iota(jnp.int32, (4 * UNIT, HD), 0)
-            seg = r // UNIT
-            base = jnp.where(
-                seg == 0, bases[0], jnp.where(seg == 1, bases[1], jnp.where(seg == 2, bases[2], bases[3]))
-            )
-            live = base + UNIT * i + r % UNIT < length
-            seen = [pl.ds(mult(base + UNIT * i, UNIT), UNIT) for base in bases]
-            out = jnp.concatenate([om[part, :] for part in seen], axis=0)
-            tile = jnp.concatenate([ml[part, :] for part in seen], axis=0)
-            got = attend_fresh(queries, out, tile, live, length)
-            rows = pl.ds(mult(i * ROWS, ROWS), ROWS)
-            att2[rows, own_cols] = got[:ROWS]
-            as2[rows, :] = got[ROWS:]
-            att2_copy(i).start()
-
-        @pl.when((i > 0) & (i < 3))
-        def _():
-            n = i - 1
-            att2_copy(n).wait_recv()
-            rows = pl.ds(mult(n * ROWS, ROWS), ROWS)
-            part = unit_rows(n)
-            left = att2[rows, :]
-            for p, g in enumerate(order):
-                proj = jnp.dot(left, w4[g], preferred_element_type=F32) * gates(g)
-                if p % 2 == 0:
-                    held = jnp.concatenate(
-                        [xs[pl.ds(mult(base + UNIT * n, UNIT), UNIT), :] for base in bases[:2]], axis=0
-                    )
-                else:
-                    held = jnp.concatenate([rx[0, part, :], rx[1, part, :]], axis=0)
-                proj = (proj + jnp.where(p // 2 == j, held.astype(F32), 0.0)).astype(BF16)
-                for v in (0, 1):
-                    sb2[v, n * 4 + p] = proj[v * UNIT : (v + 1) * UNIT]
-                    p2_copy(n * 4 + p, v).start()
-
-        @pl.when(i > 1)
-        def _():
-            finish(i - 2)
+                    sb2[v, u, e] = proj[v * UNIT : (v + 1) * UNIT, e * BLK : (e + 1) * BLK]
+                    p2_copy(u, e, v).start()
+
+        @pl.when((u >= BEHIND) & even)
+        def _():
+            finish(u - BEHIND)
 
         return carry
 
-    lax.fori_loop(0, 4, step1, 0)
+    lax.fori_loop(0, UNITS, step1, 0)
+
+    def rest(u, carry):
+        @pl.when((u >= UNITS - BEHIND) | jnp.logical_not(even))
+        def _():
+            finish(u)
+
+        return carry
+
+    lax.fori_loop(0, UNITS, rest, 0)
 
     @pl.when(even)
     def _():
-        for i in range(UNITS):
+        for i in range(UNITS1):
             f1_copy(i).wait_send()
-        for n in range(2):
-            for p in range(4):
-                for e in (0, 1):
-                    f2_copy(n, p, e).wait()
+        for u in range(UNITS):
+            for e in (0, 1):
+                f2_copy(u, e).wait()
 
     for k in (1, 2, 3):
         md_copies[k].wait_send()
@@ -598,10 +617,13 @@
         copy.wait_send()
     for i in range(PATCH // CHUNK):
         att1_copy(i).wait_send()
-    for i in range(UNITS):
+    for i in range(UNITS1):
         for v in (0, 1):
             p1_copy(i, v).wait_send()
-            p2_copy(i, v).wait_send()
+    for u in range(UNITS):
+        for v in (0, 1):
+            for e in (0, 1):
+                p2_copy(u, e, v).wait_send()
     for i in range(2):
         att2_copy(i).wait_send()
 
@@ -643,9 +665,9 @@
             vmem((2, ROWS, SLAB), BF16),
             vmem((2 * ROWS, BLK), BF16),
             vmem((2 * ROWS, SLAB), BF16),
-            vmem((2, UNITS, UNIT, SLAB), BF16),
-            vmem((2, UNITS, UNIT, SLAB), BF16),
-            vmem((UNITS, UNIT, SLAB), BF16),
+            vmem((2, UNITS, 2, UNIT, BLK), BF16),
+            vmem((2, UNITS, 2, UNIT, BLK), BF16),
+            vmem((UNITS, 2, UNIT, BLK), BF16),
             pltpu.SMEM((NP,), jnp.int32),
             dma((21,)),
             dma((3,)),
@@ -656,20 +678,20 @@
             dma((8,)),
             dma((PATCH // CHUNK,)),
             dma((PATCH // CHUNK,)),
-            dma((2, UNITS)),
-            dma((2, UNITS)),
-            dma((UNITS,)),
-            dma((UNITS,)),
+            dma((2, UNITS1)),
+            dma((2, UNITS1)),
+            dma((UNITS1,)),
+            dma((UNITS1,)),
             dma((3, chunks)),
             dma((3, chunks)),
             dma((2,)),
             dma((2,)),
             dma((2,)),
             dma((2,)),
-            dma((2, UNITS)),
-            dma((2, UNITS)),
-            dma((2, UNITS)),
-            dma((2, UNITS)),
+            dma((2, UNITS, 2)),
+            dma((2, UNITS, 2)),
+            dma((UNITS, 2)),
+            dma((UNITS, 2)),
         ],
         compiler_params=pltpu.CompilerParams(
             collective_id=0, has_side_effects=True, vmem_limit_bytes=40 << 20

time: 63 us -> 60.6 us (0.962)
  Pallas kernels: 61.4 us -> 59 us
    pallas_call x1, Pallas kernels: 61.4 us -> 59 us  [shards(): pl.pallas_call(functools.partial(kernel, n_pipe), out_shape=jax.ShapeDtyp...]
where the time goes in v4:
time: 60.6 us; the launch traced here: 60.4 us
  Pallas kernels  59 us (97%)
  local copies, waits for them, and re-layouts  0.75 us (1%)
  between operations  0.66 us (1%)
    pallas_call x1, Pallas kernels, shards(): pl.pallas_call(functools.partial(kernel, n_pipe), out_shape=jax.ShapeDtyp...  59 us

profile of v4, /device:TPU:1, one launch (start us, length us, event | category | flops | bytes accessed | tf_op | source)
XLA Modules:
  0.0 60.4 jit_solution(4213773044795543485)
XLA Ops:
  0.7 59.0 %section_steps.1 = bf16[64,3072]{1,0:T(8,128)(2,1)S(1)} custom-call(bf16[64,3072]{1,0:T(8,128)(2,1)} %x_hbm.1, bf16[1,1024,384]{2,1,0:T(8,128)(2,1)} %k_hbm.1, bf16[1,1024,384]{2,1,0:T(8,128)(2,1)} %v_hbm.1, bf16[1,384,3072]{2,1,0:T(8,128)(2,1)} %w_hbm.1, f32[1,3072]{1,0:T(1,128)} %shift_hbm.1, f32[1,3072]{1,0:T(1,128)} %scale_hbm.1, f32[1,3072]{1,0:T(1,128)} %gate_hbm.1, ...), custom_call_target="tpu_custom_call" | custom-call | tf_op jit(solution)/shard_map/section_steps/pallas_call | solution.py:638
  59.7 0.7 %copy.14 = bf16[64,3072]{1,0:T(8,128)(2,1)} copy(bf16[64,3072]{1,0:T(8,128)(2,1)S(1)} %section_steps.1) | data formatting | bytes 786432

commit v5 on v4

--- a/solution.py
+++ b/solution.py
@@ -25,7 +25,7 @@
 UNITS = PATCH // UNIT
 UNIT1 = 32
 UNITS1 = PATCH // UNIT1
-BEHIND = 2
+AT_ONCE = 5
 CHUNK = 128
 TOTAL = 960
 WIDTH = 3072
@@ -186,7 +186,6 @@
             qb[rows, HD * h : HD * (h + 1)] = (normed * q_gain).astype(BF16)
             fh[rows, HD * h : HD * (h + 1)] = (normed * k_gain).astype(BF16)
 
-    heads(fh[own_rows, BLK:], own_rows)
     pl.semaphore_wait(bar, 6)
 
     md_copies = {}
@@ -332,6 +331,7 @@
         return jnp.concatenate([lo, hi], axis=1)
 
     first, length = patch_at(0)
+    heads(fh[own_rows, BLK:], own_rows)
     for k in (1, 2, 3):
         md_copies[k].wait_recv()
         rows = pl.ds(mult(ROWS * peer[k], ROWS), ROWS)
@@ -453,7 +453,11 @@
             held = res[v].astype(F32)
             sb1[v, rows, :] = (proj * gate1[v] + jnp.where(keep, held, 0.0)).astype(BF16)
             for u in range(CHUNK // UNIT1):
-                p1_copy(i * (CHUNK // UNIT1) + u, v).start()
+
+                @pl.when(i * (CHUNK // UNIT1) + u < AT_ONCE)
+                def _():
+                    p1_copy(i * (CHUNK // UNIT1) + u, v).start()
+
         return carry
 
     lax.fori_loop(0, PATCH // CHUNK, step0, 0)
@@ -472,6 +476,13 @@
         def _():
             taken(i - 1)
             ready(i - 1)
+
+        for u in range(AT_ONCE, UNITS1):
+
+            @pl.when(i == (u - AT_ONCE) // 2)
+            def _():
+                for v in (0, 1):
+                    p1_copy(u, v).start()
 
         done = i - 1 - (1 - odd)
 
@@ -565,39 +576,36 @@
         def _():
             att2_copy(n).wait_recv()
 
-        @pl.when(u < UNITS)
-        def _():
-            g = slab_of(u)
-            part = unit_rows(n)
-            left = att2[pl.ds(mult(n * ROWS, ROWS), ROWS), :]
-            proj = jnp.dot(left, w4[g], preferred_element_type=F32) * gates(g)
-            own = jnp.concatenate(
-                [xs[pl.ds(mult(base + UNIT * n, UNIT), UNIT), :] for base in bases[:2]], axis=0
-            )
-            his = jnp.concatenate([rx[0, part, :], rx[1, part, :]], axis=0)
-            held = jnp.where(p % 2 == 0, own.astype(F32), his.astype(F32))
-            proj = (proj + jnp.where(p // 2 == j, held, 0.0)).astype(BF16)
-            for v in (0, 1):
-                for e in (0, 1):
-                    sb2[v, u, e] = proj[v * UNIT : (v + 1) * UNIT, e * BLK : (e + 1) * BLK]
-                    p2_copy(u, e, v).start()
-
-        @pl.when((u >= BEHIND) & even)
-        def _():
-            finish(u - BEHIND)
-
-        return carry
-
-    lax.fori_loop(0, UNITS, step1, 0)
-
-    def rest(u, carry):
-        @pl.when((u >= UNITS - BEHIND) | jnp.logical_not(even))
+        g = slab_of(u)
+        part = unit_rows(n)
+        left = att2[pl.ds(mult(n * ROWS, ROWS), ROWS), :]
+        proj = jnp.dot(left, w4[g], preferred_element_type=F32) * gates(g)
+        own = jnp.concatenate(
+            [xs[pl.ds(mult(base + UNIT * n, UNIT), UNIT), :] for base in bases[:2]], axis=0
+        )
+        his = jnp.concatenate([rx[0, part, :], rx[1, part, :]], axis=0)
+        held = jnp.where(p % 2 == 0, own.astype(F32), his.astype(F32))
+        proj = (proj + jnp.where(p // 2 == j, held, 0.0)).astype(BF16)
+        for v in (0, 1):
+            for e in (0, 1):
+                sb2[v, u, e] = proj[v * UNIT : (v + 1) * UNIT, e * BLK : (e + 1) * BLK]
+                p2_copy(u, e, v).start()
+
+        @pl.when(even)
         def _():
             finish(u)
 
         return carry
 
-    lax.fori_loop(0, UNITS, rest, 0)
+    lax.fori_loop(0, UNITS, step1, 0)
+
+    @pl.when(jnp.logical_not(even))
+    def _():
+        def rest(u, carry):
+            finish(u)
+            return carry
+
+        lax.fori_loop(0, UNITS, rest, 0)
 
     @pl.when(even)
     def _():

time: 60.6 us -> 59.8 us (0.987)
  Pallas kernels: 59 us -> 58.2 us
    pallas_call x1, Pallas kernels: 59 us -> 58.2 us  [shards(): pl.pallas_call(functools.partial(kernel, n_pipe), out_shape=jax.ShapeDtyp...]
where the time goes in v5:
time: 59.8 us; the launch traced here: 59.6 us
  Pallas kernels  58.2 us (97%)
  local copies, waits for them, and re-layouts  0.75 us (1%)
  between operations  0.66 us (1%)
    pallas_call x1, Pallas kernels, shards(): pl.pallas_call(functools.partial(kernel, n_pipe), out_shape=jax.ShapeDtyp...  58.2 us

profile of v5, /device:TPU:1, one launch (start us, length us, event | category | flops | bytes accessed | tf_op | source)
XLA Modules:
  0.0 59.6 jit_solution(5569746388308981907)
XLA Ops:
  0.7 58.2 %section_steps.1 = bf16[64,3072]{1,0:T(8,128)(2,1)S(1)} custom-call(bf16[64,3072]{1,0:T(8,128)(2,1)} %x_hbm.1, bf16[1,1024,384]{2,1,0:T(8,128)(2,1)} %k_hbm.1, bf16[1,1024,384]{2,1,0:T(8,128)(2,1)} %v_hbm.1, bf16[1,384,3072]{2,1,0:T(8,128)(2,1)} %w_hbm.1, f32[1,3072]{1,0:T(1,128)} %shift_hbm.1, f32[1,3072]{1,0:T(1,128)} %scale_hbm.1, f32[1,3072]{1,0:T(1,128)} %gate_hbm.1, ...), custom_call_target="tpu_custom_call" | custom-call | tf_op jit(solution)/shard_map/section_steps/pallas_call | solution.py:646
  58.9 0.7 %copy.14 = bf16[64,3072]{1,0:T(8,128)(2,1)} copy(bf16[64,3072]{1,0:T(8,128)(2,1)S(1)} %section_steps.1) | data formatting | bytes 786432

commit v6 on v5

--- a/solution.py
+++ b/solution.py
@@ -461,7 +461,6 @@
         return carry
 
     lax.fori_loop(0, PATCH // CHUNK, step0, 0)
-    refresh(first, length)
 
     def hand_over(i, carry):
         @pl.when(i < groups)
@@ -483,6 +482,10 @@
             def _():
                 for v in (0, 1):
                     p1_copy(u, v).start()
+
+        @pl.when(i == 0)
+        def _():
+            refresh(first, length)
 
         done = i - 1 - (1 - odd)
 

time: 59.8 us -> 60 us (level)
  no operation moved by 1% of the time
where the time goes in v6:
time: 60 us; the launch traced here: 59.9 us
  Pallas kernels  58.5 us (98%)
  local copies, waits for them, and re-layouts  0.75 us (1%)
  between operations  0.66 us (1%)
    pallas_call x1, Pallas kernels, shards(): pl.pallas_call(functools.partial(kernel, n_pipe), out_shape=jax.ShapeDtyp...  58.5 us

profile of v6, /device:TPU:1, one launch (start us, length us, event | category | flops | bytes accessed | tf_op | source)
XLA Modules:
  0.0 59.9 jit_solution(6652041437375881407)
XLA Ops:
  0.7 58.5 %section_steps.1 = bf16[64,3072]{1,0:T(8,128)(2,1)S(1)} custom-call(bf16[64,3072]{1,0:T(8,128)(2,1)} %x_hbm.1, bf16[1,1024,384]{2,1,0:T(8,128)(2,1)} %k_hbm.1, bf16[1,1024,384]{2,1,0:T(8,128)(2,1)} %v_hbm.1, bf16[1,384,3072]{2,1,0:T(8,128)(2,1)} %w_hbm.1, f32[1,3072]{1,0:T(1,128)} %shift_hbm.1, f32[1,3072]{1,0:T(1,128)} %scale_hbm.1, f32[1,3072]{1,0:T(1,128)} %gate_hbm.1, ...), custom_call_target="tpu_custom_call" | custom-call | tf_op jit(solution)/shard_map/section_steps/pallas_call | solution.py:649
  59.1 0.7 %copy.14 = bf16[64,3072]{1,0:T(8,128)(2,1)} copy(bf16[64,3072]{1,0:T(8,128)(2,1)S(1)} %section_steps.1) | data formatting | bytes 786432
